TPU v7x, 32 devices: a whole 2x2x4 slice. The times are simulated.
32 devices in a mesh: narrow: 4 (over x, core), wide: 8 (over z, y).
Axes of the slice: x: 2, y: 2, z: 4, core: 2. Of those that a mesh axis runs over, the one named last changes fastest.
Arguments:
- inputs: bfloat16 [32, 2304], P('wide', 'narrow'), may hold values from -6 to 6
- decoder_bias: float32 [2304], replicated, may hold values from -3 to 3
- preactivations: bfloat16 [32, 8192], P(None, ('narrow', 'wide')), may hold values from -6 to 6
- decoder_weight: bfloat16 [8192, 2304], P(('narrow', 'wide')), may hold values from -0.125 to 0.125
Outputs:
- grad_encoder: bfloat16 [2304, 8192], P(None, ('narrow', 'wide'))
- grad_decoder: bfloat16 [8192, 2304], P(('narrow', 'wide'))
All inputs are finite; a program needn't handle non-finite values.
Results may differ from a plain program's by a relative error of at most 0.0053.
Values may be sent and summed in bfloat16 or wider, within the bound.
A program may use at most 64 MiB of HBM per device.

v0:
```python
import jax
import jax.numpy as jnp
from jax import lax
from jax.sharding import PartitionSpec as P


def shards(inputs, decoder_bias, preactivations, decoder_weight):
    halfway = lax.all_gather(inputs, "narrow", axis=1, tiled=True)
    gathered = lax.all_gather(halfway, "wide", axis=0, tiled=True)
    centered = (gathered.astype(jnp.float32) - decoder_bias).astype(jnp.bfloat16)
    hidden = jnp.maximum(preactivations, jnp.zeros_like(preactivations))
    partial_value = jnp.dot(hidden, decoder_weight, preferred_element_type=jnp.float32)
    reduced = lax.psum_scatter(partial_value, "narrow", scatter_dimension=1, tiled=True)
    reduced = lax.psum_scatter(reduced, "wide", scatter_dimension=0, tiled=True)
    columns = inputs.shape[1]
    bias_cols = lax.dynamic_slice_in_dim(decoder_bias, lax.axis_index("narrow") * columns, columns)
    residual = (reduced + bias_cols - inputs.astype(jnp.float32)).astype(jnp.bfloat16)
    resid_half = lax.all_gather(residual, "narrow", axis=1, tiled=True)
    resid_whole = lax.all_gather(resid_half, "wide", axis=0, tiled=True)
    grad_decoder = jnp.einsum(
        "bf,bd->fd", hidden, resid_whole, preferred_element_type=jnp.float32
    ).astype(jnp.bfloat16)
    backward = jnp.einsum(
        "bd,fd->bf", resid_whole, decoder_weight, preferred_element_type=jnp.float32
    )
    masked = jnp.where(preactivations > 0, backward, jnp.zeros_like(backward)).astype(jnp.bfloat16)
    grad_encoder = jnp.einsum(
        "bd,bf->df", centered, masked, preferred_element_type=jnp.float32
    ).astype(jnp.bfloat16)
    return (grad_encoder, grad_decoder)


def solution(mesh):
    placed = (P("wide", "narrow"), P(), P(None, ("narrow", "wide")), P(("narrow", "wide"), None))
    return jax.shard_map(
        shards,
        mesh=mesh,
        in_specs=placed,
        out_specs=(P(None, ("narrow", "wide")), P(("narrow", "wide"), None)),
        check_vma=False,
    )
```

profile of v0, /device:TPU:0, one launch (start us, length us, event | category | flops | bytes accessed | tf_op | source)
XLA Modules:
  0.0 160.4 jit_solution(5888088555615980768)
XLA Ops:
  7.2 0.0 copy-start
  7.2 0.0 reduce-scatter.4.cloned.1.call-start
  7.2 1.2 copy-done
  8.4 2.3 %convolution_bitcast_fusion = f32[2304,32]{1,0:T(8,128)} fusion(bf16[256,2304]{1,0:T(8,128)(2,1)S(1)} %copy-done, bf16[32,256]{1,0:T(8,128)(2,1)} %param.6), kind=kOutput, calls=%fused_computation.2 | convolution fusion | flops 37756928 | bytes 1490944
  10.8 0.0 reduce-scatter.4.cloned.1.call-update
  10.8 0.0 copy-start.1
  10.8 0.0 all-reduce.3.cloned.1.call-start
  10.9 28.8 %reduce-scatter.4.cloned.1.call-done = f32[576,32]{1,0:T(8,128)} async-done(((f32[2304,32]{1,0:T(8,128)}), f32[576,32]{1,0:T(8,128)}) %reduce-scatter.4.cloned.1.call-update) | async-done | bytes 73744
  39.6 1.7 %copy.11 = f32[32,576]{1,0:T(8,128)} copy(f32[32,576]{0,1:T(8,128)} %bitcast.25) | data formatting | bytes 147456
  41.4 0.0 all-reduce.3.cloned.1.call-update
  41.4 5.2 %all-gather = bf16[4,576,4]{1,2,0:T(4,128)(2,1)S(1)} all-gather(bf16[1,576,4]{1,2,0:T(4,128)(2,1)S(1)} %bitcast.28), channel_id=1, replica_groups=mesh['narrow'=4,'wide'=8] {'narrow'}, dimensions={0}, use_global_device_ids=true | all-gather | bytes 23040 | tf_op jit(solution)/shard_map/all_gather | solution.py:8
  46.6 0.1 reshape.7
  46.7 30.7 %all-gather.1 = bf16[8,4,2304]{2,1,0:T(4,128)(2,1)S(1)} all-gather(bf16[1,4,2304]{2,1,0:T(4,128)(2,1)S(1)} %bitcast.26), channel_id=1, replica_groups=mesh['narrow'=4,'wide'=8] {'wide'}, dimensions={0}, use_global_device_ids=true | all-gather | bytes 165888 | tf_op jit(solution)/shard_map/all_gather | solution.py:9
  77.4 0.6 dynamic-slice
  78.6 0.0 copy-done.2
  78.7 0.1 dynamic_slice.3
  78.7 34.2 %all-reduce.3.cloned.1.call-done = f32[32,576]{1,0:T(8,128)} async-done(((f32[32,576]{1,0:T(8,128)}), f32[32,576]{1,0:T(8,128)}) %all-reduce.3.cloned.1.call-update) | async-done | bytes 73744
  112.9 0.7 fusion.11
  113.6 5.2 %all-gather.2 = bf16[4,576,4]{1,2,0:T(4,128)(2,1)S(1)} all-gather(bf16[1,576,4]{1,2,0:T(4,128)(2,1)S(1)} %fusion.11), channel_id=1, replica_groups=mesh['narrow'=4,'wide'=8] {'narrow'}, dimensions={0}, use_global_device_ids=true | all-gather | bytes 23040 | tf_op jit(solution)/shard_map/all_gather | solution.py:18
  118.9 0.1 reshape.11
  118.9 30.6 %all-gather.3 = bf16[8,4,2304]{2,1,0:T(4,128)(2,1)S(1)} all-gather(bf16[1,4,2304]{2,1,0:T(4,128)(2,1)S(1)} %bitcast.27), channel_id=1, replica_groups=mesh['narrow'=4,'wide'=8] {'wide'}, dimensions={0}, use_global_device_ids=true | all-gather | bytes 165888 | tf_op jit(solution)/shard_map/all_gather | solution.py:19
  149.5 0.0 copy-done.1
  149.6 1.5 convolution_convert_fusion
  151.1 2.5 %convolution_convert_fusion.1 = bf16[2304,256]{1,0:T(8,128)(2,1)} fusion(bf16[32,2304]{1,0:T(8,128)(2,1)S(1)} %reshape.13, bf16[256,2304]{1,0:T(8,128)(2,1)S(1)} %copy-done, f32[32,2304]{1,0:T(8,128)S(1)} %reshape.14, f32[2304]{0:T(1024)S(1)} %copy-done.2, bf16[32,256]{1,0:T(8,128)(2,1)S(1)} %copy-done.1), kind=kOutput, calls=%fused_computation.1 | convolution fusion | flops 76259328 | bytes 2827264 | tf_op jit(solution)/shard_map/bd,bf->df/dot_general | solution.py:27
  (9 shorter events, 0.1 us)
Async XLA Ops:
  7.2 1.3 copy-start
  7.2 32.4 %reduce-scatter.4.cloned.1.call-start = ((), (), s32[]{:S(2)}) async-start(), calls=%async_computation.1 | async-start | bytes 1474560
  10.8 30.6 %copy-start.3 = (bf16[4,576]{1,0:T(4,128)(2,1)S(1)}, bf16[4,576]{1,0:T(4,128)(2,1)}, u32[]{:S(2)}) copy-start(bf16[4,576]{1,0:T(4,128)(2,1)} %param.4) | copy-start | bytes 13828
  10.8 66.6 %copy-start.4 = (u32[32]{0:T(128)S(1)}, u32[32]{0:T(128)}, u32[]{:S(2)}) copy-start(u32[32]{0:T(128)} %constant.18) | copy-start | bytes 388
  10.8 67.9 %copy-start.2 = (f32[2304]{0:T(1024)S(1)}, f32[2304]{0:T(1024)}, u32[]{:S(2)}) copy-start(f32[2304]{0:T(1024)} %param.5) | copy-start | bytes 27652
  10.8 138.8 %copy-start.1 = (bf16[32,256]{1,0:T(8,128)(2,1)S(1)}, bf16[32,256]{1,0:T(8,128)(2,1)}, u32[]{:S(2)}) copy-start(bf16[32,256]{1,0:T(8,128)(2,1)} %param.6) | copy-start | bytes 49156
  10.8 102.1 %all-reduce.3.cloned.1.call-start = ((), (), s32[]{:S(2)}) async-start(), calls=%async_computation.2 | async-start | bytes 163840
Sparse Core Ops, SparseCore 0:
  11.2 28.4 reduce-scatter.3
  44.0 68.8 all-reduce.2
where the time goes:
time: 161 us; the launch traced here: 160 us
  blocking collectives  71.6 us (44%)
  waiting for transfers between devices  63 us (39%)
  between operations  14.8 us (9%)
  matrix products  6.31 us (4%)
  local copies, waits for them, and re-layouts  3.9 us (2%)
    unnamed x4, waiting for transfers between devices  63 us
    all_gather x1, blocking collectives, shards(): gathered = lax.all_gather(halfway, 'wide', axis=0, tiled=True)  30.7 us
    all_gather x1, blocking collectives, shards(): resid_whole = lax.all_gather(resid_half, 'wide', axis=0, tiled=True)  30.6 us
    all_gather x1, blocking collectives, shards(): halfway = lax.all_gather(inputs, 'narrow', axis=1, tiled=True)  5.19 us
    all_gather x1, blocking collectives, shards(): resid_half = lax.all_gather(residual, 'narrow', axis=1, tiled=True)  5.19 us
    unnamed x15, local copies, waits for them, and re-layouts  3.78 us
  transfers between devices with their start and end apart: 2, of which 2 were waited for; matrix products, arithmetic and copies ran while one was open for 0% of the time, Pallas kernels for 0%

commit v1 on v0

v1 whole, which is shorter than its diff:
```python
import functools

import jax
import jax.numpy as jnp
from jax import lax
from jax.experimental import pallas as pl
from jax.experimental.pallas import tpu as pltpu
from jax.sharding import PartitionSpec as P

MESH = pl.DeviceIdType.MESH
LANES = 128
BF16 = jnp.bfloat16
F32 = jnp.float32


def each(low, high, body):
    if high - low <= 16:
        for i in range(low, high):
            body(i)
    else:
        lax.fori_loop(low, high, lambda i, _: (body(i), 0)[1], 0)


def wait_bytes(ref, sem):
    pltpu.make_async_copy(ref, ref, sem).wait()


def exchange(narrow, wide, pieces, in_ref, bias_ref, pre_ref, w_hbm, resid_ref, cent_ref,
             w_ref, blocks, whole, mine, theirs, part, landed, res,
             w_sem, in_send, in_recv, inx_send, inx_recv, px_send, px_recv,
             part_send, part_recv, res_send, res_recv, rx_send, rx_recv):
    n, w = lax.axis_index("narrow"), lax.axis_index("wide")
    core, chip = n % 2, (n // 2) * wide + w
    other = 1 - core
    chips = (narrow // 2) * wide
    rows, width = whole.shape
    half = width // 2
    cols = half // LANES
    tall = part.shape[1]
    block_rows, block_cols = in_ref.shape
    stride, shift = chips // pieces, core * (chips // 2)

    def device(c):
        return {"narrow": (c // wide) * 2 + core, "wide": c % wide}

    partner = {"narrow": (n // 2) * 2 + other, "wide": w}
    place = (chip + chips - shift) % chips
    owner = (place % stride == 0) & (place // stride < pieces)
    own = lax.min(place // stride, pieces - 1)

    barrier = pltpu.get_barrier_semaphore()
    pl.semaphore_signal(barrier, inc=1, device_id=partner, device_id_type=MESH)
    each(1, chips, lambda i: pl.semaphore_signal(
        barrier, inc=1, device_id=device((chip + i) % chips), device_id_type=MESH))

    def load(h, slot):
        span = pl.ds(pl.multiple_of(h * half, LANES), half)
        return pltpu.make_async_copy(w_hbm.at[:, span], w_ref.at[slot], w_sem.at[slot])

    load(other, 0).start()
    load(core, 1).start()
    blocks[core, chip] = in_ref[...]
    pl.semaphore_wait(barrier, chips)

    def send_block(i):
        pltpu.make_async_remote_copy(
            src_ref=in_ref, dst_ref=blocks.at[core, chip], send_sem=in_send, recv_sem=in_recv,
            device_id=device((chip + i) % chips), device_id_type=MESH).start()

    each(1, chips, send_block)

    hidden = jnp.maximum(pre_ref[...], jnp.zeros_like(pre_ref))
    load(other, 0).wait()
    mine[...] = jnp.dot(hidden, w_ref[0], preferred_element_type=F32)
    swap = pltpu.make_async_remote_copy(
        src_ref=mine, dst_ref=theirs, send_sem=px_send, recv_sem=px_recv,
        device_id=partner, device_id_type=MESH)
    swap.start()
    load(core, 1).wait()
    total = jnp.dot(hidden, w_ref[1], preferred_element_type=F32)
    swap.wait()
    total = (total + theirs[...]).astype(BF16)
    for k in range(pieces):
        q, j = k // cols, k % cols
        part[k] = total[q * tall:(q + 1) * tall, j * LANES:(j + 1) * LANES]

    def send_part(i):
        k = (chip + i) % pieces
        to = (k * stride + shift) % chips

        @pl.when(to != chip)
        def _():
            pltpu.make_async_remote_copy(
                src_ref=part.at[k], dst_ref=landed.at[chip], send_sem=part_send, recv_sem=part_recv,
                device_id=device(to), device_id_type=MESH).start()

    each(0, pieces, send_part)

    wait_bytes(blocks.at[core, pl.ds(0, chips - 1)], in_recv)
    forward = pltpu.make_async_remote_copy(
        src_ref=blocks.at[core], dst_ref=blocks.at[core], send_sem=inx_send, recv_sem=inx_recv,
        device_id=partner, device_id_type=MESH)
    forward.start()
    wait_bytes(blocks.at[core, pl.ds(0, chips - 1)], in_send)
    forward.wait()
    for a in range(narrow):
        for b in range(wide):
            whole[b * block_rows:(b + 1) * block_rows, a * block_cols:(a + 1) * block_cols] = (
                blocks[a % 2, (a // 2) * wide + b].astype(F32))
    cent_ref[...] = (whole[...] - bias_ref[...]).astype(BF16)

    @pl.when(owner)
    def _():
        landed[chip] = part[own]
        wait_bytes(landed.at[pl.ds(0, chips - 1)], part_recv)
        reduced = jnp.sum(landed[...].astype(F32), axis=0)
        at = pl.ds(pl.multiple_of(core * half + (own % cols) * LANES, LANES), LANES)
        down = pl.ds(pl.multiple_of((own // cols) * tall, 16), tall)
        res[core, own] = (reduced + bias_ref[:, at] - whole[down, at]).astype(BF16)

        def send_res(i):
            pltpu.make_async_remote_copy(
                src_ref=res.at[core, own], dst_ref=res.at[core, own], send_sem=res_send,
                recv_sem=res_recv, device_id=device((chip + i) % chips),
                device_id_type=MESH).start()

        each(1, chips, send_res)
        wait_bytes(part.at[pl.ds(0, pieces - 1)], part_send)
        wait_bytes(res.at[core, pl.ds(0, pieces - 1)], res_recv)

    @pl.when(jnp.logical_not(owner))
    def _():
        wait_bytes(part, part_send)
        wait_bytes(res.at[core], res_recv)

    last = pltpu.make_async_remote_copy(
        src_ref=res.at[core], dst_ref=res.at[core], send_sem=rx_send, recv_sem=rx_recv,
        device_id=partner, device_id_type=MESH)
    last.start()

    @pl.when(owner)
    def _():
        wait_bytes(landed.at[pl.ds(0, chips - 1)], res_send)

    last.wait()
    for h in range(2):
        for k in range(pieces):
            q, j = k // cols, k % cols
            at = h * half + j * LANES
            resid_ref[q * tall:(q + 1) * tall, at:at + LANES] = res[h, k]


def gradients(pre_ref, resid_ref, cent_ref, w_hbm, enc_hbm, dec_hbm, w_ref, enc, dec, w_sem, enc_sem, dec_sem):
    load = pltpu.make_async_copy(w_hbm, w_ref, w_sem)
    load.start()
    width = resid_ref.shape[1]
    cuts = dec_sem.shape[0]
    step = width // cuts
    pre = pre_ref[...]
    hidden = jnp.maximum(pre, jnp.zeros_like(pre))
    rows_first = (((0,), (0,)), ((), ()))
    copies = []
    for i in range(cuts):
        span = slice(i * step, (i + 1) * step)
        dec[:, span] = lax.dot_general(
            hidden, resid_ref[:, span], rows_first, preferred_element_type=F32).astype(BF16)
        copies.append(pltpu.make_async_copy(dec.at[:, span], dec_hbm.at[:, span], dec_sem.at[i]))
        copies[-1].start()
    load.wait()
    backward = lax.dot_general(
        resid_ref[...], w_ref[...], (((1,), (1,)), ((), ())), preferred_element_type=F32)
    masked = jnp.where(pre.astype(F32) > 0, backward, 0.0).astype(BF16)
    for i in range(cuts):
        span = slice(i * step, (i + 1) * step)
        enc[span, :] = lax.dot_general(
            cent_ref[:, span], masked, rows_first, preferred_element_type=F32).astype(BF16)
        copies.append(pltpu.make_async_copy(enc.at[span, :], enc_hbm.at[span, :], enc_sem.at[i]))
        copies[-1].start()
    for copy in copies:
        copy.wait()


def shards(narrow, wide, inputs, decoder_bias, preactivations, decoder_weight):
    rows, features = preactivations.shape
    width = decoder_weight.shape[1]
    half, chips = width // 2, (narrow // 2) * wide
    cols = half // LANES
    groups = 1
    while cols * groups * 2 <= chips and rows % (groups * 2 * 16) == 0:
        groups *= 2
    pieces, tall = cols * groups, rows // groups
    vmem, hbm = pl.BlockSpec(memory_space=pltpu.VMEM), pl.BlockSpec(memory_space=pl.ANY)
    dma = pltpu.SemaphoreType.DMA
    whole = jax.ShapeDtypeStruct((rows, width), BF16)
    resid, centered = pl.pallas_call(
        functools.partial(exchange, narrow, wide, pieces),
        out_shape=(whole, whole),
        in_specs=[vmem, vmem, vmem, hbm],
        out_specs=(vmem, vmem),
        scratch_shapes=[
            pltpu.VMEM((2, features, half), BF16),
            pltpu.VMEM((2, chips) + inputs.shape, BF16),
            pltpu.VMEM((rows, width), F32),
            pltpu.VMEM((rows, half), F32),
            pltpu.VMEM((rows, half), F32),
            pltpu.VMEM((pieces, tall, LANES), BF16),
            pltpu.VMEM((chips, tall, LANES), BF16),
            pltpu.VMEM((2, pieces, tall, LANES), BF16),
            dma((2,)),
        ] + [dma] * 12,
        compiler_params=pltpu.CompilerParams(
            collective_id=0, has_side_effects=True, vmem_limit_bytes=32 * 2**20),
        name="exchange",
    )(inputs, decoder_bias.reshape(1, width), preactivations, decoder_weight)
    cuts = 3
    return pl.pallas_call(
        gradients,
        out_shape=(jax.ShapeDtypeStruct((width, features), BF16),
                   jax.ShapeDtypeStruct((features, width), BF16)),
        in_specs=[vmem, vmem, vmem, hbm],
        out_specs=(hbm, hbm),
        scratch_shapes=[
            pltpu.VMEM((features, width), BF16),
            pltpu.VMEM((width, features), BF16),
            pltpu.VMEM((features, width), BF16),
            dma, dma((cuts,)), dma((cuts,)),
        ],
        compiler_params=pltpu.CompilerParams(vmem_limit_bytes=32 * 2**20),
        name="gradients",
    )(preactivations, resid, centered, decoder_weight)


def solution(mesh):
    placed = (P("wide", "narrow"), P(), P(None, ("narrow", "wide")), P(("narrow", "wide"), None))
    return jax.shard_map(
        functools.partial(shards, mesh.shape["narrow"], mesh.shape["wide"]),
        mesh=mesh,
        in_specs=placed,
        out_specs=(P(None, ("narrow", "wide")), P(("narrow", "wide"), None)),
        check_vma=False,
    )
```

time: 161 us -> 26.1 us (0.16)
  blocking collectives: 71.6 us -> 0 us
  waiting for transfers between devices: 63 us -> 0 us
  Pallas kernels: 0 us -> 21.7 us
  between operations: 14.8 us -> 0.65 us
  matrix products: 6.31 us -> 0 us
    all_gather x4 -> x0, blocking collectives: 71.6 us -> none  [the longest x1 30.7 us: shards(): gathered = lax.all_gather(halfway, 'wide', axis=0, tiled=True)]
    unnamed x4 -> x0, waiting for transfers between devices: 63 us -> none
    pallas_call x0 -> x2, Pallas kernels: none -> 21.7 us  [the longest x1 18.7 us: shards(): pl.pallas_call(functools.partial(exchange, narrow, wide, pieces), out_sha...]
    dot_general x2 -> x0, matrix products: 3.98 us -> none  [the longest x1 2.47 us: shards(): jnp.einsum('bd,bf->df', centered, masked, preferred_element_type=jnp.floa...]
    unnamed x1 -> x0, matrix products: 2.33 us -> none
    unnamed x15 -> x8, local copies, waits for them, and re-layouts: 3.78 us -> 2.68 us
  transfers between devices with their start and end apart: 2 -> 0, of which waited for: 2 -> 0; matrix products, arithmetic and copies ran while one was open for 0% -> 0% of each run, Pallas kernels for 0% -> 0%
where the time goes in v1:
time: 26.1 us; the launch traced here: 25.8 us
  Pallas kernels  21.7 us (83%)
  local copies, waits for them, and re-layouts  3.39 us (13%)
  between operations  0.65 us (2%)
    pallas_call x1, Pallas kernels, shards(): pl.pallas_call(functools.partial(exchange, narrow, wide, pieces), out_sha...  18.7 us
    pallas_call x1, Pallas kernels, shards(): pl.pallas_call(gradients, out_shape=(jax.ShapeDtypeStruct((width, feature...  3.03 us
    unnamed x8, local copies, waits for them, and re-layouts  2.68 us
    reshape x1, local copies, waits for them, and re-layouts, shards(): decoder_bias.reshape(1, width)  0.71 us

profile of v1, /device:TPU:0, one launch (start us, length us, event | category | flops | bytes accessed | tf_op | source)
XLA Modules:
  0.0 25.8 jit_solution(7046059947687227339)
XLA Ops:
  0.6 0.7 %reshape.7.bias_ref = f32[1,2304]{1,0:T(1,128)S(1)} reshape(f32[2304]{0:T(1024)} %param.5) | data formatting | bytes 18432 | tf_op jit(solution)/shard_map/reshape | solution.py:214
  1.3 0.0 copy-start
  1.3 1.3 %copy-done = bf16[256,2304]{1,0:T(8,128)(2,1)S(1)} copy-done((bf16[256,2304]{1,0:T(8,128)(2,1)S(1)}, bf16[256,2304]{1,0:T(8,128)(2,1)}, u32[]{:S(2)}) %copy-start) | copy-done | bytes 1179672
  2.6 0.0 copy-start.2
  2.6 0.7 %copy-done.2 = bf16[32,256]{1,0:T(8,128)(2,1)S(1)} copy-done((bf16[32,256]{1,0:T(8,128)(2,1)S(1)}, bf16[32,256]{1,0:T(8,128)(2,1)}, u32[]{:S(2)}) %copy-start.2) | copy-done | bytes 16408
  3.3 0.0 copy-start.3
  3.3 0.7 %copy-done.3 = bf16[4,576]{1,0:T(4,128)(2,1)S(1)} copy-done((bf16[4,576]{1,0:T(4,128)(2,1)S(1)}, bf16[4,576]{1,0:T(4,128)(2,1)}, u32[]{:S(2)}) %copy-start.3) | copy-done | bytes 4632
  4.0 0.0 copy-start.1
  4.0 18.7 %exchange.1 = (bf16[32,2304]{1,0:T(8,128)(2,1)S(1)}, bf16[32,2304]{1,0:T(8,128)(2,1)S(1)}) custom-call(bf16[4,576]{1,0:T(4,128)(2,1)S(1)} %copy-done.3, f32[1,2304]{1,0:T(1,128)S(1)} %reshape.7.bias_ref, bf16[32,256]{1,0:T(8,128)(2,1)S(1)} %copy-done.2, bf16[256,2304]{1,0:T(8,128)(2,1)S(1)} %copy-done), custom_call_target="tpu_custom_call" | custom-call | tf_op jit(solution)/shard_map/exchange/pallas_call | solution.py:195
  22.8 0.0 copy-done.1
  22.8 3.0 %gradients.1 = (bf16[2304,256]{1,0:T(8,128)(2,1)}, bf16[256,2304]{1,0:T(8,128)(2,1)}) custom-call(bf16[32,256]{1,0:T(8,128)(2,1)S(1)} %copy-done.2, bf16[32,2304]{1,0:T(8,128)(2,1)S(1)} %get-tuple-element.4.resid_ref, bf16[32,2304]{1,0:T(8,128)(2,1)S(1)} %get-tuple-element.5.cent_ref, bf16[256,2304]{1,0:T(8,128)(2,1)S(1)} %copy-done.1), custom_call_target="tpu_custom_call" | custom-call | tf_op jit(solution)/shard_map/gradients/pallas_call | solution.py:216
Async XLA Ops:
  1.3 1.3 %copy-start = (bf16[256,2304]{1,0:T(8,128)(2,1)S(1)}, bf16[256,2304]{1,0:T(8,128)(2,1)}, u32[]{:S(2)}) copy-start(bf16[256,2304]{1,0:T(8,128)(2,1)} %w_hbm.3) | copy-start | bytes 3538948
  2.6 0.7 %copy-start.2 = (bf16[32,256]{1,0:T(8,128)(2,1)S(1)}, bf16[32,256]{1,0:T(8,128)(2,1)}, u32[]{:S(2)}) copy-start(bf16[32,256]{1,0:T(8,128)(2,1)} %pre_ref.3) | copy-start | bytes 49156
  3.3 0.7 %copy-start.3 = (bf16[4,576]{1,0:T(4,128)(2,1)S(1)}, bf16[4,576]{1,0:T(4,128)(2,1)}, u32[]{:S(2)}) copy-start(bf16[4,576]{1,0:T(4,128)(2,1)} %in_ref.1) | copy-start | bytes 13828
  4.0 18.7 %copy-start.1 = (bf16[256,2304]{1,0:T(8,128)(2,1)S(1)}, bf16[256,2304]{1,0:T(8,128)(2,1)}, u32[]{:S(2)}) copy-start(bf16[256,2304]{1,0:T(8,128)(2,1)} %w_hbm.3) | copy-start | bytes 3538948

commit v2 on v1

v2 whole, which is shorter than its diff:
```python
import functools

import jax
import jax.numpy as jnp
from jax import lax
from jax.experimental import pallas as pl
from jax.experimental.pallas import tpu as pltpu
from jax.sharding import PartitionSpec as P

MESH = pl.DeviceIdType.MESH
LANES = 128
BF16 = jnp.bfloat16
F32 = jnp.float32


def each(low, high, body):
    if high - low <= 16:
        for i in range(low, high):
            body(i)
    else:
        lax.fori_loop(low, high, lambda i, _: (body(i), 0)[1], 0)


def wait_bytes(ref, sem):
    pltpu.make_async_copy(ref, ref, sem).wait()


def exchange(narrow, wide, pieces, in_hbm, bias_hbm, pre_hbm, w_hbm, resid_ref, cent_ref, hid_ref,
             w_ref, in_ref, pre_ref, flat, bias_ref, band, blocks, whole, mine, theirs, part, landed, res,
             w_sem, in_sem, pre_sem, bias_sem, in_send, in_recv, inx_send, inx_recv, px_send, px_recv,
             part_send, part_recv, res_send, res_recv, rx_send, rx_recv):
    n, w = lax.axis_index("narrow"), lax.axis_index("wide")
    core, chip = n % 2, (n // 2) * wide + w
    other = 1 - core
    chips = (narrow // 2) * wide
    rows, width = whole.shape
    half = width // 2
    cols = half // LANES
    tall = part.shape[1]
    block_rows, block_cols = in_ref.shape
    stride, shift = chips // pieces, core * (chips // 2)

    def device(c):
        return {"narrow": (c // wide) * 2 + core, "wide": c % wide}

    partner = {"narrow": (n // 2) * 2 + other, "wide": w}
    place = (chip + chips - shift) % chips
    owner = (place % stride == 0) & (place // stride < pieces)
    own = lax.min(place // stride, pieces - 1)

    def columns(h):
        return pl.ds(pl.multiple_of(h * half, LANES), half)

    def load(h, slot):
        return pltpu.make_async_copy(w_hbm.at[:, columns(h)], w_ref.at[slot], w_sem.at[slot])

    small = [pltpu.make_async_copy(in_hbm, in_ref, in_sem),
             pltpu.make_async_copy(pre_hbm, pre_ref, pre_sem),
             pltpu.make_async_copy(bias_hbm, flat, bias_sem)]
    for copy in small:
        copy.start()
    load(other, 0).start()
    load(core, 1).start()

    barrier = pltpu.get_barrier_semaphore()
    pl.semaphore_signal(barrier, inc=1, device_id=partner, device_id_type=MESH)
    each(1, chips, lambda i: pl.semaphore_signal(
        barrier, inc=1, device_id=device((chip + i) % chips), device_id_type=MESH))

    for copy in small:
        copy.wait()
    block = in_ref[...]
    blocks[core, chip] = block
    bias_ref[...] = flat[...].reshape(1, width)
    for a in range(narrow):
        for b in range(8 // block_rows):
            band[b * block_rows:(b + 1) * block_rows, a * block_cols:(a + 1) * block_cols] = block.astype(F32)

    def placed(h):
        repeated = jnp.concatenate([band[:, columns(h)]] * (rows // 8), axis=0)
        row = lax.broadcasted_iota(jnp.int32, (rows, half), 0) - w * block_rows
        col = lax.broadcasted_iota(jnp.int32, (rows, half), 1) + (h * half - n * block_cols)
        inside = (row >= 0) & (row < block_rows) & (col >= 0) & (col < block_cols)
        return jnp.where(inside, repeated, 0.0)

    hidden = jnp.maximum(pre_ref[...], jnp.zeros_like(pre_ref))
    load(other, 0).wait()
    mine[...] = jnp.dot(hidden, w_ref[0], preferred_element_type=F32) - placed(other)
    pl.semaphore_wait(barrier, chips)
    swap = pltpu.make_async_remote_copy(
        src_ref=mine, dst_ref=theirs, send_sem=px_send, recv_sem=px_recv,
        device_id=partner, device_id_type=MESH)
    swap.start()

    def send_block(i):
        pltpu.make_async_remote_copy(
            src_ref=in_ref, dst_ref=blocks.at[core, chip], send_sem=in_send, recv_sem=in_recv,
            device_id=device((chip + i) % chips), device_id_type=MESH).start()

    each(1, chips, send_block)
    load(core, 1).wait()
    total = jnp.dot(hidden, w_ref[1], preferred_element_type=F32) - placed(core)
    swap.wait_recv()
    total = (total + theirs[...]).astype(BF16)
    for k in range(pieces):
        q, j = k // cols, k % cols
        part[k] = total[q * tall:(q + 1) * tall, j * LANES:(j + 1) * LANES]

    def send_part(i):
        k = (chip + i) % pieces
        to = (k * stride + shift) % chips

        @pl.when(to != chip)
        def _():
            pltpu.make_async_remote_copy(
                src_ref=part.at[k], dst_ref=landed.at[chip], send_sem=part_send, recv_sem=part_recv,
                device_id=device(to), device_id_type=MESH).start()

    each(0, pieces, send_part)

    @pl.when(owner)
    def _():
        landed[chip] = part[own]
        wait_bytes(landed.at[pl.ds(0, chips - 1)], part_recv)
        reduced = jnp.sum(landed[...].astype(F32), axis=0)
        at = pl.ds(pl.multiple_of(core * half + (own % cols) * LANES, LANES), LANES)
        res[core, own] = (reduced + bias_ref[:, at]).astype(BF16)

        def send_res(i):
            pltpu.make_async_remote_copy(
                src_ref=res.at[core, own], dst_ref=res.at[core, own], send_sem=res_send,
                recv_sem=res_recv, device_id=device((chip + i) % chips),
                device_id_type=MESH).start()

        each(1, chips, send_res)

    wait_bytes(blocks.at[core, pl.ds(0, chips - 1)], in_recv)
    forward = pltpu.make_async_remote_copy(
        src_ref=blocks.at[core], dst_ref=blocks.at[core], send_sem=inx_send, recv_sem=inx_recv,
        device_id=partner, device_id_type=MESH)
    forward.start()
    hid_ref[...] = hidden.astype(F32).T.astype(BF16)
    forward.wait_recv()
    for a in range(narrow):
        for b in range(wide):
            whole[b * block_rows:(b + 1) * block_rows, a * block_cols:(a + 1) * block_cols] = (
                blocks[a % 2, (a // 2) * wide + b].astype(F32))
    cent_ref[...] = (whole[...] - bias_ref[...]).T.astype(BF16)

    @pl.when(owner)
    def _():
        wait_bytes(res.at[core, pl.ds(0, pieces - 1)], res_recv)

    @pl.when(jnp.logical_not(owner))
    def _():
        wait_bytes(res.at[core], res_recv)

    last = pltpu.make_async_remote_copy(
        src_ref=res.at[core], dst_ref=res.at[core], send_sem=rx_send, recv_sem=rx_recv,
        device_id=partner, device_id_type=MESH)
    last.start()
    swap.wait_send()
    forward.wait_send()
    wait_bytes(blocks.at[core, pl.ds(0, chips - 1)], in_send)

    @pl.when(owner)
    def _():
        wait_bytes(part.at[pl.ds(0, pieces - 1)], part_send)
        wait_bytes(landed.at[pl.ds(0, chips - 1)], res_send)

    @pl.when(jnp.logical_not(owner))
    def _():
        wait_bytes(part, part_send)

    last.wait()
    for h in range(2):
        for k in range(pieces):
            q, j = k // cols, k % cols
            at = h * half + j * LANES
            resid_ref[q * tall:(q + 1) * tall, at:at + LANES] = res[h, k]


def gradients(pre_ref, hid_ref, resid_ref, cent_ref, w_ref, enc_hbm, dec_hbm, enc, dec, enc_sem, dec_sem):
    width = resid_ref.shape[1]
    cuts = dec_sem.shape[0]
    step = width // cuts
    copies = []
    for i in range(cuts):
        span = slice(i * step, (i + 1) * step)
        dec[:, span] = jnp.dot(
            hid_ref[...], resid_ref[:, span], preferred_element_type=F32).astype(BF16)
        copies.append(pltpu.make_async_copy(dec.at[:, span], dec_hbm.at[:, span], dec_sem.at[i]))
        copies[-1].start()
    backward = lax.dot_general(
        resid_ref[...], w_ref[...], (((1,), (1,)), ((), ())), preferred_element_type=F32)
    masked = jnp.where(pre_ref[...].astype(F32) > 0, backward, 0.0).astype(BF16)
    for i in range(cuts):
        span = slice(i * step, (i + 1) * step)
        enc[span, :] = jnp.dot(
            cent_ref[span, :], masked, preferred_element_type=F32).astype(BF16)
        copies.append(pltpu.make_async_copy(enc.at[span, :], enc_hbm.at[span, :], enc_sem.at[i]))
        copies[-1].start()
    for copy in copies:
        copy.wait()


def shards(narrow, wide, inputs, decoder_bias, preactivations, decoder_weight):
    rows, features = preactivations.shape
    width = decoder_weight.shape[1]
    half, chips = width // 2, (narrow // 2) * wide
    cols = half // LANES
    groups = 1
    while cols * groups * 2 <= chips and rows % (groups * 2 * 16) == 0:
        groups *= 2
    pieces, tall = cols * groups, rows // groups
    vmem, hbm = pl.BlockSpec(memory_space=pltpu.VMEM), pl.BlockSpec(memory_space=pltpu.HBM)
    dma = pltpu.SemaphoreType.DMA
    resid, centered, hidden = pl.pallas_call(
        functools.partial(exchange, narrow, wide, pieces),
        out_shape=(jax.ShapeDtypeStruct((rows, width), BF16),
                   jax.ShapeDtypeStruct((width, rows), BF16),
                   jax.ShapeDtypeStruct((features, rows), BF16)),
        in_specs=[hbm] * 4,
        out_specs=(vmem,) * 3,
        scratch_shapes=[
            pltpu.VMEM((2, features, half), BF16),
            pltpu.VMEM(inputs.shape, BF16),
            pltpu.VMEM((rows, features), BF16),
            pltpu.VMEM((width,), F32),
            pltpu.VMEM((1, width), F32),
            pltpu.VMEM((8, width), F32),
            pltpu.VMEM((2, chips) + inputs.shape, BF16),
            pltpu.VMEM((rows, width), F32),
            pltpu.VMEM((rows, half), F32),
            pltpu.VMEM((rows, half), F32),
            pltpu.VMEM((pieces, tall, LANES), BF16),
            pltpu.VMEM((chips, tall, LANES), BF16),
            pltpu.VMEM((2, pieces, tall, LANES), BF16),
            dma((2,)),
        ] + [dma] * 15,
        compiler_params=pltpu.CompilerParams(
            collective_id=0, has_side_effects=True, vmem_limit_bytes=32 * 2**20),
        name="exchange",
    )(*(pltpu.with_memory_space_constraint(x, pltpu.HBM)
        for x in (inputs, decoder_bias, preactivations, decoder_weight)))
    cuts = 3
    return pl.pallas_call(
        gradients,
        out_shape=(jax.ShapeDtypeStruct((width, features), BF16),
                   jax.ShapeDtypeStruct((features, width), BF16)),
        in_specs=[vmem] * 5,
        out_specs=(hbm, hbm),
        scratch_shapes=[
            pltpu.VMEM((width, features), BF16),
            pltpu.VMEM((features, width), BF16),
            dma((cuts,)), dma((cuts,)),
        ],
        compiler_params=pltpu.CompilerParams(vmem_limit_bytes=32 * 2**20),
        name="gradients",
    )(preactivations, hidden, resid, centered, decoder_weight)


def solution(mesh):
    placed = (P("wide", "narrow"), P(), P(None, ("narrow", "wide")), P(("narrow", "wide"), None))
    return jax.shard_map(
        functools.partial(shards, mesh.shape["narrow"], mesh.shape["wide"]),
        mesh=mesh,
        in_specs=placed,
        out_specs=(P(None, ("narrow", "wide")), P(("narrow", "wide"), None)),
        check_vma=False,
    )
```

time: 26.1 us -> 21.7 us (0.83)
  local copies, waits for them, and re-layouts: 3.39 us -> 0.01 us
  Pallas kernels: 21.7 us -> 20.9 us
    unnamed x8 -> x4, local copies, waits for them, and re-layouts: 2.68 us -> 0.01 us
    reshape x1 -> x0, local copies, waits for them, and re-layouts: 0.71 us -> none  [shards(): decoder_bias.reshape(1, width)]
    pallas_call x1, Pallas kernels: 3.03 us -> 2.55 us  [shards(): pl.pallas_call(gradients, out_shape=(jax.ShapeDtypeStruct((width, feature...]
    pallas_call x1, Pallas kernels: 18.7 us -> 18.3 us  [shards(): pl.pallas_call(functools.partial(exchange, narrow, wide, pieces), out_sha...]
where the time goes in v2:
time: 21.7 us; the launch traced here: 21.6 us
  Pallas kernels  20.9 us (96%)
  between operations  0.67 us (3%)
    pallas_call x1, Pallas kernels, shards(): pl.pallas_call(functools.partial(exchange, narrow, wide, pieces), out_sha...  18.3 us
    pallas_call x1, Pallas kernels, shards(): pl.pallas_call(gradients, out_shape=(jax.ShapeDtypeStruct((width, feature...  2.55 us

profile of v2, /device:TPU:0, one launch (start us, length us, event | category | flops | bytes accessed | tf_op | source)
XLA Modules:
  0.0 21.6 jit_solution(17774129632341461682)
XLA Ops:
  0.6 0.0 copy-start
  0.6 0.0 copy-start.1
  0.7 18.3 %exchange.1 = (bf16[32,2304]{1,0:T(8,128)(2,1)S(1)}, bf16[2304,32]{1,0:T(8,128)(2,1)S(1)}, bf16[256,32]{1,0:T(8,128)(2,1)S(1)}) custom-call(bf16[4,576]{1,0:T(4,128)(2,1)} %in_hbm.1, f32[2304]{0:T(1024)} %bias_hbm.1, bf16[32,256]{1,0:T(8,128)(2,1)} %pre_ref.1, bf16[256,2304]{1,0:T(8,128)(2,1)} %w_ref.1), custom_call_target="tpu_custom_call" | custom-call | tf_op jit(solution)/shard_map/exchange/pallas_call | solution.py:218
  19.0 0.0 copy-done
  19.0 0.0 copy-done.1
  19.0 2.6 %gradients.1 = (bf16[2304,256]{1,0:T(8,128)(2,1)}, bf16[256,2304]{1,0:T(8,128)(2,1)}) custom-call(bf16[32,256]{1,0:T(8,128)(2,1)S(1)} %copy-done.1, bf16[256,32]{1,0:T(8,128)(2,1)S(1)} %get-tuple-element.5.hid_ref, bf16[32,2304]{1,0:T(8,128)(2,1)S(1)} %get-tuple-element.6.resid_ref, bf16[2304,32]{1,0:T(8,128)(2,1)S(1)} %get-tuple-element.7.cent_ref, ...), custom_call_target="tpu_custom_call" | custom-call | tf_op jit(solution)/shard_map/gradients/pallas_call | solution.py:247
Async XLA Ops:
  0.6 18.4 %copy-start = (bf16[256,2304]{1,0:T(8,128)(2,1)S(1)}, bf16[256,2304]{1,0:T(8,128)(2,1)}, u32[]{:S(2)}) copy-start(bf16[256,2304]{1,0:T(8,128)(2,1)} %w_ref.1) | copy-start | bytes 3538948
  0.6 18.4 %copy-start.1 = (bf16[32,256]{1,0:T(8,128)(2,1)S(1)}, bf16[32,256]{1,0:T(8,128)(2,1)}, u32[]{:S(2)}) copy-start(bf16[32,256]{1,0:T(8,128)(2,1)} %pre_ref.1) | copy-start | bytes 49156

commit v3 on v2

--- a/solution.py
+++ b/solution.py
@@ -21,32 +21,56 @@
         lax.fori_loop(low, high, lambda i, _: (body(i), 0)[1], 0)
 
 
+def div(a, b):
+    return a // b if isinstance(a, int) else a if b == 1 else lax.div(a, jnp.int32(b))
+
+
+def rem(a, b):
+    return a % b if isinstance(a, int) else lax.rem(a, jnp.int32(b))
+
+
 def wait_bytes(ref, sem):
     pltpu.make_async_copy(ref, ref, sem).wait()
 
 
-def exchange(narrow, wide, pieces, in_hbm, bias_hbm, pre_hbm, w_hbm, resid_ref, cent_ref, hid_ref,
+def exchange(narrow, wide, pieces, in_hbm, bias_hbm, pre_hbm, w_hbm, resid_ref, cent_ref, hid_ref, dec_ref, back_ref,
              w_ref, in_ref, pre_ref, flat, bias_ref, band, blocks, whole, mine, theirs, part, landed, res,
              w_sem, in_sem, pre_sem, bias_sem, in_send, in_recv, inx_send, inx_recv, px_send, px_recv,
              part_send, part_recv, res_send, res_recv, rx_send, rx_recv):
     n, w = lax.axis_index("narrow"), lax.axis_index("wide")
-    core, chip = n % 2, (n // 2) * wide + w
-    other = 1 - core
-    chips = (narrow // 2) * wide
+    core, pair = rem(n, 2), div(n, 2)
+    other, chip, pairs = 1 - core, pair * wide + w, narrow // 2
+    chips = pairs * wide
     rows, width = whole.shape
     half = width // 2
     cols = half // LANES
     tall = part.shape[1]
     block_rows, block_cols = in_ref.shape
-    stride, shift = chips // pieces, core * (chips // 2)
+    stride = chips // pieces
 
     def device(c):
-        return {"narrow": (c // wide) * 2 + core, "wide": c % wide}
-
-    partner = {"narrow": (n // 2) * 2 + other, "wide": w}
-    place = (chip + chips - shift) % chips
-    owner = (place % stride == 0) & (place // stride < pieces)
-    own = lax.min(place // stride, pieces - 1)
+        return {"narrow": div(c, wide) * 2 + core, "wide": rem(c, wide)}
+
+    def peers(body):
+        if chips <= 16:
+            along = [rem(pair + a, pairs) * 2 + core for a in range(pairs)]
+            across = [rem(w + b, wide) for b in range(wide)]
+            for b in range(wide):
+                for a in range(pairs):
+                    if a or b:
+                        body({"narrow": along[a], "wide": across[b]})
+        else:
+            each(1, chips, lambda i: body(device(rem(chip + i, chips))))
+
+    partner = {"narrow": pair * 2 + other, "wide": w}
+    turn = core * (pairs // 2)
+    place = rem(pair + pairs - turn, pairs) * wide + w
+    owner = (rem(place, stride) == 0) & (div(place, stride) < pieces)
+    own = lax.min(div(place, stride), pieces - 1)
+
+    def assembled(h):
+        return jnp.concatenate([jnp.concatenate([
+            res[h, q * cols + j] for j in range(cols)], axis=1) for q in range(pieces // cols)], axis=0)
 
     def columns(h):
         return pl.ds(pl.multiple_of(h * half, LANES), half)
@@ -64,8 +88,7 @@
 
     barrier = pltpu.get_barrier_semaphore()
     pl.semaphore_signal(barrier, inc=1, device_id=partner, device_id_type=MESH)
-    each(1, chips, lambda i: pl.semaphore_signal(
-        barrier, inc=1, device_id=device((chip + i) % chips), device_id_type=MESH))
+    peers(lambda to: pl.semaphore_signal(barrier, inc=1, device_id=to, device_id_type=MESH))
 
     for copy in small:
         copy.wait()
@@ -92,12 +115,12 @@
         device_id=partner, device_id_type=MESH)
     swap.start()
 
-    def send_block(i):
+    def send_block(to):
         pltpu.make_async_remote_copy(
             src_ref=in_ref, dst_ref=blocks.at[core, chip], send_sem=in_send, recv_sem=in_recv,
-            device_id=device((chip + i) % chips), device_id_type=MESH).start()
-
-    each(1, chips, send_block)
+            device_id=to, device_id_type=MESH).start()
+
+    peers(send_block)
     load(core, 1).wait()
     total = jnp.dot(hidden, w_ref[1], preferred_element_type=F32) - placed(core)
     swap.wait_recv()
@@ -106,15 +129,14 @@
         q, j = k // cols, k % cols
         part[k] = total[q * tall:(q + 1) * tall, j * LANES:(j + 1) * LANES]
 
-    def send_part(i):
-        k = (chip + i) % pieces
-        to = (k * stride + shift) % chips
-
-        @pl.when(to != chip)
+    def send_part(k):
+        row, to_wide = rem(div(k * stride, wide) + turn, pairs), rem(k * stride, wide)
+
+        @pl.when(row * wide + to_wide != chip)
         def _():
             pltpu.make_async_remote_copy(
                 src_ref=part.at[k], dst_ref=landed.at[chip], send_sem=part_send, recv_sem=part_recv,
-                device_id=device(to), device_id_type=MESH).start()
+                device_id={"narrow": row * 2 + core, "wide": to_wide}, device_id_type=MESH).start()
 
     each(0, pieces, send_part)
 
@@ -126,13 +148,12 @@
         at = pl.ds(pl.multiple_of(core * half + (own % cols) * LANES, LANES), LANES)
         res[core, own] = (reduced + bias_ref[:, at]).astype(BF16)
 
-        def send_res(i):
+        def send_res(to):
             pltpu.make_async_remote_copy(
                 src_ref=res.at[core, own], dst_ref=res.at[core, own], send_sem=res_send,
-                recv_sem=res_recv, device_id=device((chip + i) % chips),
-                device_id_type=MESH).start()
-
-        each(1, chips, send_res)
+                recv_sem=res_recv, device_id=to, device_id_type=MESH).start()
+
+        peers(send_res)
 
     wait_bytes(blocks.at[core, pl.ds(0, chips - 1)], in_recv)
     forward = pltpu.make_async_remote_copy(
@@ -159,6 +180,9 @@
         src_ref=res.at[core], dst_ref=res.at[core], send_sem=rx_send, recv_sem=rx_recv,
         device_id=partner, device_id_type=MESH)
     last.start()
+    first = assembled(core)
+    dec_ref[...] = jnp.dot(hid_ref[...], first, preferred_element_type=F32).astype(BF16)
+    back_ref[...] = lax.dot_general(first, w_ref[1], (((1,), (1,)), ((), ())), preferred_element_type=F32)
     swap.wait_send()
     forward.wait_send()
     wait_bytes(blocks.at[core, pl.ds(0, chips - 1)], in_send)
@@ -173,27 +197,27 @@
         wait_bytes(part, part_send)
 
     last.wait()
-    for h in range(2):
-        for k in range(pieces):
-            q, j = k // cols, k % cols
-            at = h * half + j * LANES
-            resid_ref[q * tall:(q + 1) * tall, at:at + LANES] = res[h, k]
-
-
-def gradients(pre_ref, hid_ref, resid_ref, cent_ref, w_ref, enc_hbm, dec_hbm, enc, dec, enc_sem, dec_sem):
-    width = resid_ref.shape[1]
-    cuts = dec_sem.shape[0]
-    step = width // cuts
-    copies = []
-    for i in range(cuts):
-        span = slice(i * step, (i + 1) * step)
-        dec[:, span] = jnp.dot(
-            hid_ref[...], resid_ref[:, span], preferred_element_type=F32).astype(BF16)
-        copies.append(pltpu.make_async_copy(dec.at[:, span], dec_hbm.at[:, span], dec_sem.at[i]))
-        copies[-1].start()
-    backward = lax.dot_general(
-        resid_ref[...], w_ref[...], (((1,), (1,)), ((), ())), preferred_element_type=F32)
+    resid_ref[...] = assembled(other)
+
+
+def gradients(hid_ref, resid_ref, cent_ref, dec_ref, back_ref, pre_ref, w_ref, enc_hbm, dec_hbm,
+              enc, dec, enc_sem, dec_sem):
+    core = rem(lax.axis_index("narrow"), 2)
+    half = resid_ref.shape[1]
+
+    def columns(h):
+        return pl.ds(pl.multiple_of(h * half, LANES), half)
+
+    copies = [pltpu.make_async_copy(dec_ref, dec_hbm.at[:, columns(core)], dec_sem.at[0])]
+    copies[0].start()
+    backward = back_ref[...] + lax.dot_general(
+        resid_ref[...], w_ref[:, columns(1 - core)], (((1,), (1,)), ((), ())), preferred_element_type=F32)
     masked = jnp.where(pre_ref[...].astype(F32) > 0, backward, 0.0).astype(BF16)
+    dec[...] = jnp.dot(hid_ref[...], resid_ref[...], preferred_element_type=F32).astype(BF16)
+    copies.append(pltpu.make_async_copy(dec, dec_hbm.at[:, columns(1 - core)], dec_sem.at[1]))
+    copies[1].start()
+    cuts = enc_sem.shape[0]
+    step = enc.shape[0] // cuts
     for i in range(cuts):
         span = slice(i * step, (i + 1) * step)
         enc[span, :] = jnp.dot(
@@ -215,13 +239,15 @@
     pieces, tall = cols * groups, rows // groups
     vmem, hbm = pl.BlockSpec(memory_space=pltpu.VMEM), pl.BlockSpec(memory_space=pltpu.HBM)
     dma = pltpu.SemaphoreType.DMA
-    resid, centered, hidden = pl.pallas_call(
+    kept = pl.pallas_call(
         functools.partial(exchange, narrow, wide, pieces),
-        out_shape=(jax.ShapeDtypeStruct((rows, width), BF16),
+        out_shape=(jax.ShapeDtypeStruct((rows, half), BF16),
                    jax.ShapeDtypeStruct((width, rows), BF16),
-                   jax.ShapeDtypeStruct((features, rows), BF16)),
+                   jax.ShapeDtypeStruct((features, rows), BF16),
+                   jax.ShapeDtypeStruct((features, half), BF16),
+                   jax.ShapeDtypeStruct((rows, features), F32)),
         in_specs=[hbm] * 4,
-        out_specs=(vmem,) * 3,
+        out_specs=(vmem,) * 5,
         scratch_shapes=[
             pltpu.VMEM((2, features, half), BF16),
             pltpu.VMEM(inputs.shape, BF16),
@@ -243,21 +269,21 @@
         name="exchange",
     )(*(pltpu.with_memory_space_constraint(x, pltpu.HBM)
         for x in (inputs, decoder_bias, preactivations, decoder_weight)))
-    cuts = 3
+    resid, centered, hidden, decoder, backward = kept
     return pl.pallas_call(
         gradients,
         out_shape=(jax.ShapeDtypeStruct((width, features), BF16),
                    jax.ShapeDtypeStruct((features, width), BF16)),
-        in_specs=[vmem] * 5,
+        in_specs=[vmem] * 7,
         out_specs=(hbm, hbm),
         scratch_shapes=[
             pltpu.VMEM((width, features), BF16),
-            pltpu.VMEM((features, width), BF16),
-            dma((cuts,)), dma((cuts,)),
+            pltpu.VMEM((features, half), BF16),
+            dma((3,)), dma((2,)),
         ],
         compiler_params=pltpu.CompilerParams(vmem_limit_bytes=32 * 2**20),
         name="gradients",
-    )(preactivations, hidden, resid, centered, decoder_weight)
+    )(hidden, resid, centered, decoder, backward, preactivations, decoder_weight)
 
 
 def solution(mesh):

time: 21.7 us -> 20.9 us (0.963)
  Pallas kernels: 20.9 us -> 20.1 us
    pallas_call x1, Pallas kernels: 2.55 us -> 2.14 us  [shards(): pl.pallas_call(gradients, out_shape=(jax.ShapeDtypeStruct((width, feature...]
    pallas_call x1, Pallas kernels: 18.3 us -> 17.9 us  [shards(): pl.pallas_call(functools.partial(exchange, narrow, wide, pieces), out_sha...]
where the time goes in v3:
time: 20.9 us; the launch traced here: 20.7 us
  Pallas kernels  20.1 us (96%)
  between operations  0.67 us (3%)
    pallas_call x1, Pallas kernels, shards(): pl.pallas_call(functools.partial(exchange, narrow, wide, pieces), out_sha...  17.9 us
    pallas_call x1, Pallas kernels, shards(): pl.pallas_call(gradients, out_shape=(jax.ShapeDtypeStruct((width, feature...  2.14 us

profile of v3, /device:TPU:0, one launch (start us, length us, event | category | flops | bytes accessed | tf_op | source)
XLA Modules:
  0.0 20.7 jit_solution(2377833315413720335)
XLA Ops:
  0.6 0.0 copy-start
  0.6 0.0 copy-start.1
  0.7 17.9 %exchange.1 = (bf16[32,1152]{1,0:T(8,128)(2,1)S(1)}, bf16[2304,32]{1,0:T(8,128)(2,1)S(1)}, bf16[256,32]{1,0:T(8,128)(2,1)S(1)}, bf16[256,1152]{1,0:T(8,128)(2,1)S(1)}, f32[32,256]{1,0:T(8,128)S(1)}) custom-call(bf16[4,576]{1,0:T(4,128)(2,1)} %in_hbm.1, f32[2304]{0:T(1024)} %bias_hbm.1, bf16[32,256]{1,0:T(8,128)(2,1)} %pre_ref.1, bf16[256,2304]{1,0:T(8,128)(2,1)} %w_ref.1), custom_call_target="tpu_custom_call" | custom-call | tf_op jit(solution)/shard_map/exchange/pallas_call | solution.py:242
  18.6 0.0 copy-done
  18.6 0.0 copy-done.1
  18.6 2.1 %gradients.1 = (bf16[2304,256]{1,0:T(8,128)(2,1)}, bf16[256,2304]{1,0:T(8,128)(2,1)}) custom-call(bf16[256,32]{1,0:T(8,128)(2,1)S(1)} %get-tuple-element.7.hid_ref, bf16[32,1152]{1,0:T(8,128)(2,1)S(1)} %get-tuple-element.8.resid_ref, bf16[2304,32]{1,0:T(8,128)(2,1)S(1)} %get-tuple-element.9.cent_ref, bf16[256,1152]{1,0:T(8,128)(2,1)S(1)} %get-tuple-element.10.dec_ref, ...), custom_call_target="tpu_custom_call" | custom-call | tf_op jit(solution)/shard_map/gradients/pallas_call | solution.py:273
Async XLA Ops:
  0.6 18.0 %copy-start = (bf16[256,2304]{1,0:T(8,128)(2,1)S(1)}, bf16[256,2304]{1,0:T(8,128)(2,1)}, u32[]{:S(2)}) copy-start(bf16[256,2304]{1,0:T(8,128)(2,1)} %w_ref.1) | copy-start | bytes 3538948
  0.6 18.0 %copy-start.1 = (bf16[32,256]{1,0:T(8,128)(2,1)S(1)}, bf16[32,256]{1,0:T(8,128)(2,1)}, u32[]{:S(2)}) copy-start(bf16[32,256]{1,0:T(8,128)(2,1)} %pre_ref.1) | copy-start | bytes 49156

commit v4 on v3

--- a/solution.py
+++ b/solution.py
@@ -87,13 +87,15 @@
     load(core, 1).start()
 
     barrier = pltpu.get_barrier_semaphore()
-    pl.semaphore_signal(barrier, inc=1, device_id=partner, device_id_type=MESH)
+    for a in range(pairs):
+        pl.semaphore_signal(barrier, inc=1, device_id_type=MESH, device_id={
+            "narrow": rem(pair + a, pairs) * 2 + other, "wide": w})
     peers(lambda to: pl.semaphore_signal(barrier, inc=1, device_id=to, device_id_type=MESH))
 
     for copy in small:
         copy.wait()
     block = in_ref[...]
-    blocks[core, chip] = block
+    blocks[n, w] = block
     bias_ref[...] = flat[...].reshape(1, width)
     for a in range(narrow):
         for b in range(8 // block_rows):
@@ -109,18 +111,18 @@
     hidden = jnp.maximum(pre_ref[...], jnp.zeros_like(pre_ref))
     load(other, 0).wait()
     mine[...] = jnp.dot(hidden, w_ref[0], preferred_element_type=F32) - placed(other)
-    pl.semaphore_wait(barrier, chips)
+    pl.semaphore_wait(barrier, chips - 1 + pairs)
     swap = pltpu.make_async_remote_copy(
         src_ref=mine, dst_ref=theirs, send_sem=px_send, recv_sem=px_recv,
         device_id=partner, device_id_type=MESH)
     swap.start()
 
-    def send_block(to):
+    def send_block(b):
         pltpu.make_async_remote_copy(
-            src_ref=in_ref, dst_ref=blocks.at[core, chip], send_sem=in_send, recv_sem=in_recv,
-            device_id=to, device_id_type=MESH).start()
-
-    peers(send_block)
+            src_ref=in_ref, dst_ref=blocks.at[n, w], send_sem=in_send, recv_sem=in_recv,
+            device_id={"narrow": n, "wide": rem(w + b, wide)}, device_id_type=MESH).start()
+
+    each(1, wide, send_block)
     load(core, 1).wait()
     total = jnp.dot(hidden, w_ref[1], preferred_element_type=F32) - placed(core)
     swap.wait_recv()
@@ -139,6 +141,15 @@
                 device_id={"narrow": row * 2 + core, "wide": to_wide}, device_id_type=MESH).start()
 
     each(0, pieces, send_part)
+    wait_bytes(blocks.at[n, pl.ds(0, wide - 1)], in_recv)
+
+    def send_blocks(a):
+        pltpu.make_async_remote_copy(
+            src_ref=blocks.at[n], dst_ref=blocks.at[n], send_sem=inx_send, recv_sem=inx_recv,
+            device_id={"narrow": rem(n + a, narrow), "wide": w}, device_id_type=MESH).start()
+
+    each(1, narrow, send_blocks)
+    hid_ref[...] = hidden.astype(F32).T.astype(BF16)
 
     @pl.when(owner)
     def _():
@@ -155,17 +166,11 @@
 
         peers(send_res)
 
-    wait_bytes(blocks.at[core, pl.ds(0, chips - 1)], in_recv)
-    forward = pltpu.make_async_remote_copy(
-        src_ref=blocks.at[core], dst_ref=blocks.at[core], send_sem=inx_send, recv_sem=inx_recv,
-        device_id=partner, device_id_type=MESH)
-    forward.start()
-    hid_ref[...] = hidden.astype(F32).T.astype(BF16)
-    forward.wait_recv()
+    wait_bytes(blocks.at[pl.ds(0, narrow - 1)], inx_recv)
     for a in range(narrow):
         for b in range(wide):
             whole[b * block_rows:(b + 1) * block_rows, a * block_cols:(a + 1) * block_cols] = (
-                blocks[a % 2, (a // 2) * wide + b].astype(F32))
+                blocks[a, b].astype(F32))
     cent_ref[...] = (whole[...] - bias_ref[...]).T.astype(BF16)
 
     @pl.when(owner)
@@ -184,8 +189,8 @@
     dec_ref[...] = jnp.dot(hid_ref[...], first, preferred_element_type=F32).astype(BF16)
     back_ref[...] = lax.dot_general(first, w_ref[1], (((1,), (1,)), ((), ())), preferred_element_type=F32)
     swap.wait_send()
-    forward.wait_send()
-    wait_bytes(blocks.at[core, pl.ds(0, chips - 1)], in_send)
+    wait_bytes(blocks.at[n, pl.ds(0, wide - 1)], in_send)
+    wait_bytes(blocks.at[pl.ds(0, narrow - 1)], inx_send)
 
     @pl.when(owner)
     def _():
@@ -255,7 +260,7 @@
             pltpu.VMEM((width,), F32),
             pltpu.VMEM((1, width), F32),
             pltpu.VMEM((8, width), F32),
-            pltpu.VMEM((2, chips) + inputs.shape, BF16),
+            pltpu.VMEM((narrow, wide) + inputs.shape, BF16),
             pltpu.VMEM((rows, width), F32),
             pltpu.VMEM((rows, half), F32),
             pltpu.VMEM((rows, half), F32),

time: 20.9 us -> 20.3 us (0.971)
  Pallas kernels: 20.1 us -> 19.5 us
    pallas_call x1, Pallas kernels: 17.9 us -> 17.4 us  [shards(): pl.pallas_call(functools.partial(exchange, narrow, wide, pieces), out_sha...]
where the time goes in v4:
time: 20.3 us; the launch traced here: 20.2 us
  Pallas kernels  19.5 us (96%)
  between operations  0.67 us (3%)
    pallas_call x1, Pallas kernels, shards(): pl.pallas_call(functools.partial(exchange, narrow, wide, pieces), out_sha...  17.4 us
    pallas_call x1, Pallas kernels, shards(): pl.pallas_call(gradients, out_shape=(jax.ShapeDtypeStruct((width, feature...  2.14 us

profile of v4, /device:TPU:0, one launch (start us, length us, event | category | flops | bytes accessed | tf_op | source)
XLA Modules:
  0.0 20.2 jit_solution(10004404585308735857)
XLA Ops:
  0.6 0.0 copy-start
  0.6 0.0 copy-start.1
  0.7 17.4 %exchange.1 = (bf16[32,1152]{1,0:T(8,128)(2,1)S(1)}, bf16[2304,32]{1,0:T(8,128)(2,1)S(1)}, bf16[256,32]{1,0:T(8,128)(2,1)S(1)}, bf16[256,1152]{1,0:T(8,128)(2,1)S(1)}, f32[32,256]{1,0:T(8,128)S(1)}) custom-call(bf16[4,576]{1,0:T(4,128)(2,1)} %in_hbm.1, f32[2304]{0:T(1024)} %bias_hbm.1, bf16[32,256]{1,0:T(8,128)(2,1)} %pre_ref.1, bf16[256,2304]{1,0:T(8,128)(2,1)} %w_ref.1), custom_call_target="tpu_custom_call" | custom-call | tf_op jit(solution)/shard_map/exchange/pallas_call | solution.py:247
  18.0 0.0 copy-done
  18.0 0.0 copy-done.1
  18.0 2.1 %gradients.1 = (bf16[2304,256]{1,0:T(8,128)(2,1)}, bf16[256,2304]{1,0:T(8,128)(2,1)}) custom-call(bf16[256,32]{1,0:T(8,128)(2,1)S(1)} %get-tuple-element.7.hid_ref, bf16[32,1152]{1,0:T(8,128)(2,1)S(1)} %get-tuple-element.8.resid_ref, bf16[2304,32]{1,0:T(8,128)(2,1)S(1)} %get-tuple-element.9.cent_ref, bf16[256,1152]{1,0:T(8,128)(2,1)S(1)} %get-tuple-element.10.dec_ref, ...), custom_call_target="tpu_custom_call" | custom-call | tf_op jit(solution)/shard_map/gradients/pallas_call | solution.py:278
Async XLA Ops:
  0.6 17.4 %copy-start = (bf16[256,2304]{1,0:T(8,128)(2,1)S(1)}, bf16[256,2304]{1,0:T(8,128)(2,1)}, u32[]{:S(2)}) copy-start(bf16[256,2304]{1,0:T(8,128)(2,1)} %w_ref.1) | copy-start | bytes 3538948
  0.6 17.4 %copy-start.1 = (bf16[32,256]{1,0:T(8,128)(2,1)S(1)}, bf16[32,256]{1,0:T(8,128)(2,1)}, u32[]{:S(2)}) copy-start(bf16[32,256]{1,0:T(8,128)(2,1)} %pre_ref.1) | copy-start | bytes 49156

commit v5 on v4

--- a/solution.py
+++ b/solution.py
@@ -34,7 +34,7 @@
 
 
 def exchange(narrow, wide, pieces, in_hbm, bias_hbm, pre_hbm, w_hbm, resid_ref, cent_ref, hid_ref, dec_ref, back_ref,
-             w_ref, in_ref, pre_ref, flat, bias_ref, band, blocks, whole, mine, theirs, part, landed, res,
+             w_ref, in_ref, pre_ref, flat, bias_ref, band, blocks, whole, mine, kept, theirs, part, landed, res,
              w_sem, in_sem, pre_sem, bias_sem, in_send, in_recv, inx_send, inx_recv, px_send, px_recv,
              part_send, part_recv, res_send, res_recv, rx_send, rx_recv):
     n, w = lax.axis_index("narrow"), lax.axis_index("wide")
@@ -46,10 +46,9 @@
     cols = half // LANES
     tall = part.shape[1]
     block_rows, block_cols = in_ref.shape
-    stride = chips // pieces
-
-    def device(c):
-        return {"narrow": div(c, wide) * 2 + core, "wide": rem(c, wide)}
+    depth, edge = wide // 2, wide // 4
+    owners = pairs * depth
+    rounds = -(-pieces // owners)
 
     def peers(body):
         if chips <= 16:
@@ -58,15 +57,26 @@
             for b in range(wide):
                 for a in range(pairs):
                     if a or b:
-                        body({"narrow": along[a], "wide": across[b]})
+                        body({"narrow": along[a], "wide": across[b]}, a, b)
         else:
-            each(1, chips, lambda i: body(device(rem(chip + i, chips))))
+            def one(i):
+                a, b = div(i, wide), rem(i, wide)
+                body({"narrow": rem(pair + a, pairs) * 2 + core, "wide": rem(w + b, wide)}, a, b)
+            each(1, chips, one)
 
     partner = {"narrow": pair * 2 + other, "wide": w}
     turn = core * (pairs // 2)
-    place = rem(pair + pairs - turn, pairs) * wide + w
-    owner = (rem(place, stride) == 0) & (div(place, stride) < pieces)
-    own = lax.min(div(place, stride), pieces - 1)
+    middle = (w >= edge) & (w < edge + depth)
+    seat = rem(pair + pairs - turn, pairs) * depth + lax.min(lax.max(w - edge, 0), depth - 1)
+    held = [middle & (seat + r * owners < pieces) for r in range(rounds)]
+    owned = [lax.min(seat + r * owners, pieces - 1) for r in range(rounds)]
+
+    def by_count(body):
+        for count in range(rounds + 1):
+            at_least = held[count - 1] if count else None
+            below = jnp.logical_not(held[count]) if count < rounds else None
+            both = below if at_least is None else at_least if below is None else at_least & below
+            pl.when(both)(functools.partial(body, count))
 
     def assembled(h):
         return jnp.concatenate([jnp.concatenate([
@@ -90,7 +100,18 @@
     for a in range(pairs):
         pl.semaphore_signal(barrier, inc=1, device_id_type=MESH, device_id={
             "narrow": rem(pair + a, pairs) * 2 + other, "wide": w})
-    peers(lambda to: pl.semaphore_signal(barrier, inc=1, device_id=to, device_id_type=MESH))
+
+    def greet(to, a, b):
+        def signal():
+            pl.semaphore_signal(barrier, inc=1, device_id=to, device_id_type=MESH)
+
+        if isinstance(a, int) and (a == 0 or b == 0):
+            signal()
+        else:
+            there = (to["wide"] >= edge) & (to["wide"] < edge + depth)
+            pl.when(middle | there | (a == 0) | (b == 0))(signal)
+
+    peers(greet)
 
     for copy in small:
         copy.wait()
@@ -111,7 +132,17 @@
     hidden = jnp.maximum(pre_ref[...], jnp.zeros_like(pre_ref))
     load(other, 0).wait()
     mine[...] = jnp.dot(hidden, w_ref[0], preferred_element_type=F32) - placed(other)
-    pl.semaphore_wait(barrier, chips - 1 + pairs)
+    load(core, 1).wait()
+    kept[...] = jnp.dot(hidden, w_ref[1], preferred_element_type=F32) - placed(core)
+
+    @pl.when(middle)
+    def _():
+        pl.semaphore_wait(barrier, pairs + chips - 1)
+
+    @pl.when(jnp.logical_not(middle))
+    def _():
+        pl.semaphore_wait(barrier, pairs + owners + wide - depth - 1 + pairs - 1)
+
     swap = pltpu.make_async_remote_copy(
         src_ref=mine, dst_ref=theirs, send_sem=px_send, recv_sem=px_recv,
         device_id=partner, device_id_type=MESH)
@@ -123,21 +154,20 @@
             device_id={"narrow": n, "wide": rem(w + b, wide)}, device_id_type=MESH).start()
 
     each(1, wide, send_block)
-    load(core, 1).wait()
-    total = jnp.dot(hidden, w_ref[1], preferred_element_type=F32) - placed(core)
     swap.wait_recv()
-    total = (total + theirs[...]).astype(BF16)
+    total = (kept[...] + theirs[...]).astype(BF16)
     for k in range(pieces):
         q, j = k // cols, k % cols
         part[k] = total[q * tall:(q + 1) * tall, j * LANES:(j + 1) * LANES]
 
     def send_part(k):
-        row, to_wide = rem(div(k * stride, wide) + turn, pairs), rem(k * stride, wide)
+        spot, r = rem(k, owners), div(k, owners)
+        row, to_wide = rem(div(spot, depth) + turn, pairs), edge + rem(spot, depth)
 
         @pl.when(row * wide + to_wide != chip)
         def _():
             pltpu.make_async_remote_copy(
-                src_ref=part.at[k], dst_ref=landed.at[chip], send_sem=part_send, recv_sem=part_recv,
+                src_ref=part.at[k], dst_ref=landed.at[r, chip], send_sem=part_send, recv_sem=part_recv.at[r],
                 device_id={"narrow": row * 2 + core, "wide": to_wide}, device_id_type=MESH).start()
 
     each(0, pieces, send_part)
@@ -151,20 +181,23 @@
     each(1, narrow, send_blocks)
     hid_ref[...] = hidden.astype(F32).T.astype(BF16)
 
-    @pl.when(owner)
-    def _():
-        landed[chip] = part[own]
-        wait_bytes(landed.at[pl.ds(0, chips - 1)], part_recv)
-        reduced = jnp.sum(landed[...].astype(F32), axis=0)
-        at = pl.ds(pl.multiple_of(core * half + (own % cols) * LANES, LANES), LANES)
+    def finish(r):
+        own = owned[r]
+        landed[r, chip] = part[own]
+        wait_bytes(landed.at[r, pl.ds(0, chips - 1)], part_recv.at[r])
+        reduced = jnp.sum(landed[r].astype(F32), axis=0)
+        at = pl.ds(pl.multiple_of(core * half + rem(own, cols) * LANES, LANES), LANES)
         res[core, own] = (reduced + bias_ref[:, at]).astype(BF16)
 
-        def send_res(to):
+        def send_res(to, a, b):
             pltpu.make_async_remote_copy(
-                src_ref=res.at[core, own], dst_ref=res.at[core, own], send_sem=res_send,
+                src_ref=res.at[core, own], dst_ref=res.at[core, own], send_sem=res_send.at[r],
                 recv_sem=res_recv, device_id=to, device_id_type=MESH).start()
 
         peers(send_res)
+
+    for r in range(rounds):
+        pl.when(held[r])(functools.partial(finish, r))
 
     wait_bytes(blocks.at[pl.ds(0, narrow - 1)], inx_recv)
     for a in range(narrow):
@@ -173,14 +206,7 @@
                 blocks[a, b].astype(F32))
     cent_ref[...] = (whole[...] - bias_ref[...]).T.astype(BF16)
 
-    @pl.when(owner)
-    def _():
-        wait_bytes(res.at[core, pl.ds(0, pieces - 1)], res_recv)
-
-    @pl.when(jnp.logical_not(owner))
-    def _():
-        wait_bytes(res.at[core], res_recv)
-
+    by_count(lambda count: wait_bytes(res.at[core, pl.ds(0, pieces - count)], res_recv))
     last = pltpu.make_async_remote_copy(
         src_ref=res.at[core], dst_ref=res.at[core], send_sem=rx_send, recv_sem=rx_recv,
         device_id=partner, device_id_type=MESH)
@@ -192,15 +218,10 @@
     wait_bytes(blocks.at[n, pl.ds(0, wide - 1)], in_send)
     wait_bytes(blocks.at[pl.ds(0, narrow - 1)], inx_send)
 
-    @pl.when(owner)
-    def _():
-        wait_bytes(part.at[pl.ds(0, pieces - 1)], part_send)
-        wait_bytes(landed.at[pl.ds(0, chips - 1)], res_send)
-
-    @pl.when(jnp.logical_not(owner))
-    def _():
-        wait_bytes(part, part_send)
-
+    by_count(lambda count: wait_bytes(part.at[pl.ds(0, pieces - count)], part_send))
+    for r in range(rounds):
+        pl.when(held[r])(functools.partial(
+            wait_bytes, landed.at[r, pl.ds(0, chips - 1)], res_send.at[r]))
     last.wait()
     resid_ref[...] = assembled(other)
 
@@ -242,6 +263,7 @@
     while cols * groups * 2 <= chips and rows % (groups * 2 * 16) == 0:
         groups *= 2
     pieces, tall = cols * groups, rows // groups
+    rounds = -(-pieces // (narrow // 2 * (wide // 2)))
     vmem, hbm = pl.BlockSpec(memory_space=pltpu.VMEM), pl.BlockSpec(memory_space=pltpu.HBM)
     dma = pltpu.SemaphoreType.DMA
     kept = pl.pallas_call(
@@ -264,11 +286,12 @@
             pltpu.VMEM((rows, width), F32),
             pltpu.VMEM((rows, half), F32),
             pltpu.VMEM((rows, half), F32),
+            pltpu.VMEM((rows, half), F32),
             pltpu.VMEM((pieces, tall, LANES), BF16),
-            pltpu.VMEM((chips, tall, LANES), BF16),
+            pltpu.VMEM((rounds, chips, tall, LANES), BF16),
             pltpu.VMEM((2, pieces, tall, LANES), BF16),
             dma((2,)),
-        ] + [dma] * 15,
+        ] + [dma] * 10 + [dma((rounds,)), dma((rounds,)), dma, dma, dma],
         compiler_params=pltpu.CompilerParams(
             collective_id=0, has_side_effects=True, vmem_limit_bytes=32 * 2**20),
         name="exchange",

time: 20.3 us -> 19.9 us (0.980)
  Pallas kernels: 19.5 us -> 19 us
    pallas_call x1, Pallas kernels: 17.4 us -> 16.9 us  [shards(): pl.pallas_call(functools.partial(exchange, narrow, wide, pieces), out_sha...]
where the time goes in v5:
time: 19.9 us; the launch traced here: 19.7 us
  Pallas kernels  19 us (95%)
  between operations  0.67 us (3%)
    pallas_call x1, Pallas kernels, shards(): pl.pallas_call(functools.partial(exchange, narrow, wide, pieces), out_sha...  16.9 us
    pallas_call x1, Pallas kernels, shards(): pl.pallas_call(gradients, out_shape=(jax.ShapeDtypeStruct((width, feature...  2.14 us

profile of v5, /device:TPU:0, one launch (start us, length us, event | category | flops | bytes accessed | tf_op | source)
XLA Modules:
  0.0 19.7 jit_solution(7498834056376714560)
XLA Ops:
  0.6 0.0 copy-start
  0.6 0.0 copy-start.1
  0.7 16.9 %exchange.1 = (bf16[32,1152]{1,0:T(8,128)(2,1)S(1)}, bf16[2304,32]{1,0:T(8,128)(2,1)S(1)}, bf16[256,32]{1,0:T(8,128)(2,1)S(1)}, bf16[256,1152]{1,0:T(8,128)(2,1)S(1)}, f32[32,256]{1,0:T(8,128)S(1)}) custom-call(bf16[4,576]{1,0:T(4,128)(2,1)} %in_hbm.1, f32[2304]{0:T(1024)} %bias_hbm.1, bf16[32,256]{1,0:T(8,128)(2,1)} %pre_ref.1, bf16[256,2304]{1,0:T(8,128)(2,1)} %w_ref.1), custom_call_target="tpu_custom_call" | custom-call | tf_op jit(solution)/shard_map/exchange/pallas_call | solution.py:269
  17.6 0.0 copy-done
  17.6 0.0 copy-done.1
  17.6 2.1 %gradients.1 = (bf16[2304,256]{1,0:T(8,128)(2,1)}, bf16[256,2304]{1,0:T(8,128)(2,1)}) custom-call(bf16[256,32]{1,0:T(8,128)(2,1)S(1)} %get-tuple-element.7.hid_ref, bf16[32,1152]{1,0:T(8,128)(2,1)S(1)} %get-tuple-element.8.resid_ref, bf16[2304,32]{1,0:T(8,128)(2,1)S(1)} %get-tuple-element.9.cent_ref, bf16[256,1152]{1,0:T(8,128)(2,1)S(1)} %get-tuple-element.10.dec_ref, ...), custom_call_target="tpu_custom_call" | custom-call | tf_op jit(solution)/shard_map/gradients/pallas_call | solution.py:301
Async XLA Ops:
  0.6 16.9 %copy-start = (bf16[256,2304]{1,0:T(8,128)(2,1)S(1)}, bf16[256,2304]{1,0:T(8,128)(2,1)}, u32[]{:S(2)}) copy-start(bf16[256,2304]{1,0:T(8,128)(2,1)} %w_ref.1) | copy-start | bytes 3538948
  0.6 16.9 %copy-start.1 = (bf16[32,256]{1,0:T(8,128)(2,1)S(1)}, bf16[32,256]{1,0:T(8,128)(2,1)}, u32[]{:S(2)}) copy-start(bf16[32,256]{1,0:T(8,128)(2,1)} %pre_ref.1) | copy-start | bytes 49156

commit v6 on v5

--- a/solution.py
+++ b/solution.py
@@ -54,8 +54,8 @@
         if chips <= 16:
             along = [rem(pair + a, pairs) * 2 + core for a in range(pairs)]
             across = [rem(w + b, wide) for b in range(wide)]
-            for b in range(wide):
-                for a in range(pairs):
+            for b in (*range(edge + 1, wide), *range(edge + 1)):
+                for a in reversed(range(pairs)):
                     if a or b:
                         body({"narrow": along[a], "wide": across[b]}, a, b)
         else:
@@ -65,9 +65,8 @@
             each(1, chips, one)
 
     partner = {"narrow": pair * 2 + other, "wide": w}
-    turn = core * (pairs // 2)
     middle = (w >= edge) & (w < edge + depth)
-    seat = rem(pair + pairs - turn, pairs) * depth + lax.min(lax.max(w - edge, 0), depth - 1)
+    seat = pair * depth + lax.min(lax.max(w - edge, 0), depth - 1)
     held = [middle & (seat + r * owners < pieces) for r in range(rounds)]
     owned = [lax.min(seat + r * owners, pieces - 1) for r in range(rounds)]
 
@@ -87,6 +86,22 @@
 
     def load(h, slot):
         return pltpu.make_async_copy(w_hbm.at[:, columns(h)], w_ref.at[slot], w_sem.at[slot])
+
+    barrier = pltpu.get_barrier_semaphore()
+    def greet(to, a, b):
+        def signal():
+            pl.semaphore_signal(barrier, inc=1, device_id=to, device_id_type=MESH)
+
+        if isinstance(a, int) and (a == 0 or b == 0):
+            signal()
+        else:
+            there = (to["wide"] >= edge) & (to["wide"] < edge + depth)
+            pl.when(middle | there | (a == 0) | (b == 0))(signal)
+
+    peers(greet)
+    for a in range(pairs):
+        pl.semaphore_signal(barrier, inc=1, device_id_type=MESH, device_id={
+            "narrow": rem(pair + a, pairs) * 2 + other, "wide": w})
 
     small = [pltpu.make_async_copy(in_hbm, in_ref, in_sem),
              pltpu.make_async_copy(pre_hbm, pre_ref, pre_sem),
@@ -95,23 +110,6 @@
         copy.start()
     load(other, 0).start()
     load(core, 1).start()
-
-    barrier = pltpu.get_barrier_semaphore()
-    for a in range(pairs):
-        pl.semaphore_signal(barrier, inc=1, device_id_type=MESH, device_id={
-            "narrow": rem(pair + a, pairs) * 2 + other, "wide": w})
-
-    def greet(to, a, b):
-        def signal():
-            pl.semaphore_signal(barrier, inc=1, device_id=to, device_id_type=MESH)
-
-        if isinstance(a, int) and (a == 0 or b == 0):
-            signal()
-        else:
-            there = (to["wide"] >= edge) & (to["wide"] < edge + depth)
-            pl.when(middle | there | (a == 0) | (b == 0))(signal)
-
-    peers(greet)
 
     for copy in small:
         copy.wait()
@@ -131,7 +129,10 @@
 
     hidden = jnp.maximum(pre_ref[...], jnp.zeros_like(pre_ref))
     load(other, 0).wait()
-    mine[...] = jnp.dot(hidden, w_ref[0], preferred_element_type=F32) - placed(other)
+    sent = jnp.dot(hidden, w_ref[0], preferred_element_type=F32) - placed(other)
+    step = mine.shape[2]
+    for i in range(mine.shape[0]):
+        mine[i] = sent[:, i * step:(i + 1) * step]
     load(core, 1).wait()
     kept[...] = jnp.dot(hidden, w_ref[1], preferred_element_type=F32) - placed(core)
 
@@ -143,10 +144,12 @@
     def _():
         pl.semaphore_wait(barrier, pairs + owners + wide - depth - 1 + pairs - 1)
 
-    swap = pltpu.make_async_remote_copy(
-        src_ref=mine, dst_ref=theirs, send_sem=px_send, recv_sem=px_recv,
-        device_id=partner, device_id_type=MESH)
-    swap.start()
+    cuts = mine.shape[0]
+    swaps = [pltpu.make_async_remote_copy(
+        src_ref=mine.at[i], dst_ref=theirs.at[i], send_sem=px_send.at[i], recv_sem=px_recv.at[i],
+        device_id=partner, device_id_type=MESH) for i in range(cuts)]
+    for swap in swaps:
+        swap.start()
 
     def send_block(b):
         pltpu.make_async_remote_copy(
@@ -154,15 +157,9 @@
             device_id={"narrow": n, "wide": rem(w + b, wide)}, device_id_type=MESH).start()
 
     each(1, wide, send_block)
-    swap.wait_recv()
-    total = (kept[...] + theirs[...]).astype(BF16)
-    for k in range(pieces):
-        q, j = k // cols, k % cols
-        part[k] = total[q * tall:(q + 1) * tall, j * LANES:(j + 1) * LANES]
-
     def send_part(k):
         spot, r = rem(k, owners), div(k, owners)
-        row, to_wide = rem(div(spot, depth) + turn, pairs), edge + rem(spot, depth)
+        row, to_wide = div(spot, depth), edge + rem(spot, depth)
 
         @pl.when(row * wide + to_wide != chip)
         def _():
@@ -170,7 +167,14 @@
                 src_ref=part.at[k], dst_ref=landed.at[r, chip], send_sem=part_send, recv_sem=part_recv.at[r],
                 device_id={"narrow": row * 2 + core, "wide": to_wide}, device_id_type=MESH).start()
 
-    each(0, pieces, send_part)
+    for i in range(cuts):
+        swaps[i].wait_recv()
+        total = (kept[:, i * step:(i + 1) * step] + theirs[i]).astype(BF16)
+        for k in range(pieces):
+            q, j = k // cols, k % cols - i * step // LANES
+            if 0 <= j < step // LANES:
+                part[k] = total[q * tall:(q + 1) * tall, j * LANES:(j + 1) * LANES]
+                send_part(k)
     wait_bytes(blocks.at[n, pl.ds(0, wide - 1)], in_recv)
 
     def send_blocks(a):
@@ -214,7 +218,8 @@
     first = assembled(core)
     dec_ref[...] = jnp.dot(hid_ref[...], first, preferred_element_type=F32).astype(BF16)
     back_ref[...] = lax.dot_general(first, w_ref[1], (((1,), (1,)), ((), ())), preferred_element_type=F32)
-    swap.wait_send()
+    for swap in swaps:
+        swap.wait_send()
     wait_bytes(blocks.at[n, pl.ds(0, wide - 1)], in_send)
     wait_bytes(blocks.at[pl.ds(0, narrow - 1)], inx_send)
 
@@ -263,6 +268,7 @@
     while cols * groups * 2 <= chips and rows % (groups * 2 * 16) == 0:
         groups *= 2
     pieces, tall = cols * groups, rows // groups
+    cuts = 3 if cols % 3 == 0 else 1
     rounds = -(-pieces // (narrow // 2 * (wide // 2)))
     vmem, hbm = pl.BlockSpec(memory_space=pltpu.VMEM), pl.BlockSpec(memory_space=pltpu.HBM)
     dma = pltpu.SemaphoreType.DMA
@@ -284,14 +290,14 @@
             pltpu.VMEM((8, width), F32),
             pltpu.VMEM((narrow, wide) + inputs.shape, BF16),
             pltpu.VMEM((rows, width), F32),
+            pltpu.VMEM((cuts, rows, half // cuts), F32),
             pltpu.VMEM((rows, half), F32),
-            pltpu.VMEM((rows, half), F32),
-            pltpu.VMEM((rows, half), F32),
+            pltpu.VMEM((cuts, rows, half // cuts), F32),
             pltpu.VMEM((pieces, tall, LANES), BF16),
             pltpu.VMEM((rounds, chips, tall, LANES), BF16),
             pltpu.VMEM((2, pieces, tall, LANES), BF16),
             dma((2,)),
-        ] + [dma] * 10 + [dma((rounds,)), dma((rounds,)), dma, dma, dma],
+        ] + [dma] * 7 + [dma((cuts,)), dma((cuts,)), dma, dma((rounds,)), dma((rounds,)), dma, dma, dma],
         compiler_params=pltpu.CompilerParams(
             collective_id=0, has_side_effects=True, vmem_limit_bytes=32 * 2**20),
         name="exchange",

time: 19.9 us -> 19.9 us (level)
  no operation moved by 1% of the time
where the time goes in v6:
time: 19.9 us; the launch traced here: 19.7 us
  Pallas kernels  19 us (95%)
  between operations  0.67 us (3%)
    pallas_call x1, Pallas kernels, shards(): pl.pallas_call(functools.partial(exchange, narrow, wide, pieces), out_sha...  16.9 us
    pallas_call x1, Pallas kernels, shards(): pl.pallas_call(gradients, out_shape=(jax.ShapeDtypeStruct((width, feature...  2.13 us

profile of v6, /device:TPU:0, one launch (start us, length us, event | category | flops | bytes accessed | tf_op | source)
XLA Modules:
  0.0 19.7 jit_solution(15175066728458786690)
XLA Ops:
  0.6 0.0 copy-start
  0.6 0.0 copy-start.1
  0.7 16.9 %exchange.1 = (bf16[32,1152]{1,0:T(8,128)(2,1)S(1)}, bf16[2304,32]{1,0:T(8,128)(2,1)S(1)}, bf16[256,32]{1,0:T(8,128)(2,1)S(1)}, bf16[256,1152]{1,0:T(8,128)(2,1)S(1)}, f32[32,256]{1,0:T(8,128)S(1)}) custom-call(bf16[4,576]{1,0:T(4,128)(2,1)} %in_hbm.1, f32[2304]{0:T(1024)} %bias_hbm.1, bf16[32,256]{1,0:T(8,128)(2,1)} %pre_ref.1, bf16[256,2304]{1,0:T(8,128)(2,1)} %w_ref.1), custom_call_target="tpu_custom_call" | custom-call | tf_op jit(solution)/shard_map/exchange/pallas_call | solution.py:275
  17.6 0.0 copy-done
  17.6 0.0 copy-done.1
  17.6 2.1 %gradients.1 = (bf16[2304,256]{1,0:T(8,128)(2,1)}, bf16[256,2304]{1,0:T(8,128)(2,1)}) custom-call(bf16[256,32]{1,0:T(8,128)(2,1)S(1)} %get-tuple-element.7.hid_ref, bf16[32,1152]{1,0:T(8,128)(2,1)S(1)} %get-tuple-element.8.resid_ref, bf16[2304,32]{1,0:T(8,128)(2,1)S(1)} %get-tuple-element.9.cent_ref, bf16[256,1152]{1,0:T(8,128)(2,1)S(1)} %get-tuple-element.10.dec_ref, ...), custom_call_target="tpu_custom_call" | custom-call | tf_op jit(solution)/shard_map/gradients/pallas_call | solution.py:307
Async XLA Ops:
  0.6 16.9 %copy-start = (bf16[256,2304]{1,0:T(8,128)(2,1)S(1)}, bf16[256,2304]{1,0:T(8,128)(2,1)}, u32[]{:S(2)}) copy-start(bf16[256,2304]{1,0:T(8,128)(2,1)} %w_ref.1) | copy-start | bytes 3538948
  0.6 16.9 %copy-start.1 = (bf16[32,256]{1,0:T(8,128)(2,1)S(1)}, bf16[32,256]{1,0:T(8,128)(2,1)}, u32[]{:S(2)}) copy-start(bf16[32,256]{1,0:T(8,128)(2,1)} %pre_ref.1) | copy-start | bytes 49156

commit v7 on v6

--- a/solution.py
+++ b/solution.py
@@ -203,13 +203,6 @@
     for r in range(rounds):
         pl.when(held[r])(functools.partial(finish, r))
 
-    wait_bytes(blocks.at[pl.ds(0, narrow - 1)], inx_recv)
-    for a in range(narrow):
-        for b in range(wide):
-            whole[b * block_rows:(b + 1) * block_rows, a * block_cols:(a + 1) * block_cols] = (
-                blocks[a, b].astype(F32))
-    cent_ref[...] = (whole[...] - bias_ref[...]).T.astype(BF16)
-
     by_count(lambda count: wait_bytes(res.at[core, pl.ds(0, pieces - count)], res_recv))
     last = pltpu.make_async_remote_copy(
         src_ref=res.at[core], dst_ref=res.at[core], send_sem=rx_send, recv_sem=rx_recv,
@@ -218,6 +211,13 @@
     first = assembled(core)
     dec_ref[...] = jnp.dot(hid_ref[...], first, preferred_element_type=F32).astype(BF16)
     back_ref[...] = lax.dot_general(first, w_ref[1], (((1,), (1,)), ((), ())), preferred_element_type=F32)
+
+    wait_bytes(blocks.at[pl.ds(0, narrow - 1)], inx_recv)
+    for a in range(narrow):
+        for b in range(wide):
+            whole[b * block_rows:(b + 1) * block_rows, a * block_cols:(a + 1) * block_cols] = (
+                blocks[a, b].astype(F32))
+    cent_ref[...] = (whole[...] - bias_ref[...]).T.astype(BF16)
     for swap in swaps:
         swap.wait_send()
     wait_bytes(blocks.at[n, pl.ds(0, wide - 1)], in_send)

time: 19.9 us -> 19.9 us (level)
  no operation moved by 1% of the time
where the time goes in v7:
time: 19.9 us; the launch traced here: 19.7 us
  Pallas kernels  19 us (95%)
  between operations  0.67 us (3%)
    pallas_call x1, Pallas kernels, shards(): pl.pallas_call(functools.partial(exchange, narrow, wide, pieces), out_sha...  16.9 us
    pallas_call x1, Pallas kernels, shards(): pl.pallas_call(gradients, out_shape=(jax.ShapeDtypeStruct((width, feature...  2.13 us

profile of v7, /device:TPU:0, one launch (start us, length us, event | category | flops | bytes accessed | tf_op | source)
XLA Modules:
  0.0 19.7 jit_solution(11168591649107247053)
XLA Ops:
  0.6 0.0 copy-start
  0.6 0.0 copy-start.1
  0.7 16.9 %exchange.1 = (bf16[32,1152]{1,0:T(8,128)(2,1)S(1)}, bf16[2304,32]{1,0:T(8,128)(2,1)S(1)}, bf16[256,32]{1,0:T(8,128)(2,1)S(1)}, bf16[256,1152]{1,0:T(8,128)(2,1)S(1)}, f32[32,256]{1,0:T(8,128)S(1)}) custom-call(bf16[4,576]{1,0:T(4,128)(2,1)} %in_hbm.1, f32[2304]{0:T(1024)} %bias_hbm.1, bf16[32,256]{1,0:T(8,128)(2,1)} %pre_ref.1, bf16[256,2304]{1,0:T(8,128)(2,1)} %w_ref.1), custom_call_target="tpu_custom_call" | custom-call | tf_op jit(solution)/shard_map/exchange/pallas_call | solution.py:275
  17.6 0.0 copy-done
  17.6 0.0 copy-done.1
  17.6 2.1 %gradients.1 = (bf16[2304,256]{1,0:T(8,128)(2,1)}, bf16[256,2304]{1,0:T(8,128)(2,1)}) custom-call(bf16[256,32]{1,0:T(8,128)(2,1)S(1)} %get-tuple-element.7.hid_ref, bf16[32,1152]{1,0:T(8,128)(2,1)S(1)} %get-tuple-element.8.resid_ref, bf16[2304,32]{1,0:T(8,128)(2,1)S(1)} %get-tuple-element.9.cent_ref, bf16[256,1152]{1,0:T(8,128)(2,1)S(1)} %get-tuple-element.10.dec_ref, ...), custom_call_target="tpu_custom_call" | custom-call | tf_op jit(solution)/shard_map/gradients/pallas_call | solution.py:307
Async XLA Ops:
  0.6 16.9 %copy-start = (bf16[256,2304]{1,0:T(8,128)(2,1)S(1)}, bf16[256,2304]{1,0:T(8,128)(2,1)}, u32[]{:S(2)}) copy-start(bf16[256,2304]{1,0:T(8,128)(2,1)} %w_ref.1) | copy-start | bytes 3538948
  0.6 16.9 %copy-start.1 = (bf16[32,256]{1,0:T(8,128)(2,1)S(1)}, bf16[32,256]{1,0:T(8,128)(2,1)}, u32[]{:S(2)}) copy-start(bf16[32,256]{1,0:T(8,128)(2,1)} %pre_ref.1) | copy-start | bytes 49156

commit v8 on v7

--- a/solution.py
+++ b/solution.py
@@ -182,7 +182,7 @@
             src_ref=blocks.at[n], dst_ref=blocks.at[n], send_sem=inx_send, recv_sem=inx_recv,
             device_id={"narrow": rem(n + a, narrow), "wide": w}, device_id_type=MESH).start()
 
-    each(1, narrow, send_blocks)
+    pl.when(jnp.logical_not(middle))(lambda: each(1, narrow, send_blocks))
     hid_ref[...] = hidden.astype(F32).T.astype(BF16)
 
     def finish(r):
@@ -202,6 +202,7 @@
 
     for r in range(rounds):
         pl.when(held[r])(functools.partial(finish, r))
+    pl.when(middle)(lambda: each(1, narrow, send_blocks))
 
     by_count(lambda count: wait_bytes(res.at[core, pl.ds(0, pieces - count)], res_recv))
     last = pltpu.make_async_remote_copy(

time: 19.9 us -> 19.9 us (level)
  no operation moved by 1% of the time
where the time goes in v8:
time: 19.9 us; the launch traced here: 19.7 us
  Pallas kernels  19 us (95%)
  between operations  0.67 us (3%)
    pallas_call x1, Pallas kernels, shards(): pl.pallas_call(functools.partial(exchange, narrow, wide, pieces), out_sha...  16.9 us
    pallas_call x1, Pallas kernels, shards(): pl.pallas_call(gradients, out_shape=(jax.ShapeDtypeStruct((width, feature...  2.13 us

profile of v8, /device:TPU:0, one launch (start us, length us, event | category | flops | bytes accessed | tf_op | source)
XLA Modules:
  0.0 19.7 jit_solution(8255993030010625640)
XLA Ops:
  0.6 0.0 copy-start
  0.6 0.0 copy-start.1
  0.7 16.9 %exchange.1 = (bf16[32,1152]{1,0:T(8,128)(2,1)S(1)}, bf16[2304,32]{1,0:T(8,128)(2,1)S(1)}, bf16[256,32]{1,0:T(8,128)(2,1)S(1)}, bf16[256,1152]{1,0:T(8,128)(2,1)S(1)}, f32[32,256]{1,0:T(8,128)S(1)}) custom-call(bf16[4,576]{1,0:T(4,128)(2,1)} %in_hbm.1, f32[2304]{0:T(1024)} %bias_hbm.1, bf16[32,256]{1,0:T(8,128)(2,1)} %pre_ref.1, bf16[256,2304]{1,0:T(8,128)(2,1)} %w_ref.1), custom_call_target="tpu_custom_call" | custom-call | tf_op jit(solution)/shard_map/exchange/pallas_call | solution.py:276
  17.6 0.0 copy-done
  17.6 0.0 copy-done.1
  17.6 2.1 %gradients.1 = (bf16[2304,256]{1,0:T(8,128)(2,1)}, bf16[256,2304]{1,0:T(8,128)(2,1)}) custom-call(bf16[256,32]{1,0:T(8,128)(2,1)S(1)} %get-tuple-element.7.hid_ref, bf16[32,1152]{1,0:T(8,128)(2,1)S(1)} %get-tuple-element.8.resid_ref, bf16[2304,32]{1,0:T(8,128)(2,1)S(1)} %get-tuple-element.9.cent_ref, bf16[256,1152]{1,0:T(8,128)(2,1)S(1)} %get-tuple-element.10.dec_ref, ...), custom_call_target="tpu_custom_call" | custom-call | tf_op jit(solution)/shard_map/gradients/pallas_call | solution.py:308
Async XLA Ops:
  0.6 16.9 %copy-start = (bf16[256,2304]{1,0:T(8,128)(2,1)S(1)}, bf16[256,2304]{1,0:T(8,128)(2,1)}, u32[]{:S(2)}) copy-start(bf16[256,2304]{1,0:T(8,128)(2,1)} %w_ref.1) | copy-start | bytes 3538948
  0.6 16.9 %copy-start.1 = (bf16[32,256]{1,0:T(8,128)(2,1)S(1)}, bf16[32,256]{1,0:T(8,128)(2,1)}, u32[]{:S(2)}) copy-start(bf16[32,256]{1,0:T(8,128)(2,1)} %pre_ref.1) | copy-start | bytes 49156

commit v9 on v7

--- a/solution.py
+++ b/solution.py
@@ -156,7 +156,7 @@
             src_ref=in_ref, dst_ref=blocks.at[n, w], send_sem=in_send, recv_sem=in_recv,
             device_id={"narrow": n, "wide": rem(w + b, wide)}, device_id_type=MESH).start()
 
-    each(1, wide, send_block)
+
     def send_part(k):
         spot, r = rem(k, owners), div(k, owners)
         row, to_wide = div(spot, depth), edge + rem(spot, depth)
@@ -175,6 +175,7 @@
             if 0 <= j < step // LANES:
                 part[k] = total[q * tall:(q + 1) * tall, j * LANES:(j + 1) * LANES]
                 send_part(k)
+    each(1, wide, send_block)
     wait_bytes(blocks.at[n, pl.ds(0, wide - 1)], in_recv)
 
     def send_blocks(a):

time: 19.9 us -> 20.3 us (1.020)
  Pallas kernels: 19 us -> 19.5 us
    pallas_call x1, Pallas kernels: 16.9 us -> 17.4 us  [shards(): pl.pallas_call(functools.partial(exchange, narrow, wide, pieces), out_sha...]
where the time goes in v9:
time: 20.3 us; the launch traced here: 20.2 us
  Pallas kernels  19.5 us (96%)
  between operations  0.67 us (3%)
    pallas_call x1, Pallas kernels, shards(): pl.pallas_call(functools.partial(exchange, narrow, wide, pieces), out_sha...  17.4 us
    pallas_call x1, Pallas kernels, shards(): pl.pallas_call(gradients, out_shape=(jax.ShapeDtypeStruct((width, feature...  2.14 us

profile of v9, /device:TPU:0, one launch (start us, length us, event | category | flops | bytes accessed | tf_op | source)
XLA Modules:
  0.0 20.2 jit_solution(9098327854674188501)
XLA Ops:
  0.6 0.0 copy-start
  0.6 0.0 copy-start.1
  0.7 17.4 %exchange.1 = (bf16[32,1152]{1,0:T(8,128)(2,1)S(1)}, bf16[2304,32]{1,0:T(8,128)(2,1)S(1)}, bf16[256,32]{1,0:T(8,128)(2,1)S(1)}, bf16[256,1152]{1,0:T(8,128)(2,1)S(1)}, f32[32,256]{1,0:T(8,128)S(1)}) custom-call(bf16[4,576]{1,0:T(4,128)(2,1)} %in_hbm.1, f32[2304]{0:T(1024)} %bias_hbm.1, bf16[32,256]{1,0:T(8,128)(2,1)} %pre_ref.1, bf16[256,2304]{1,0:T(8,128)(2,1)} %w_ref.1), custom_call_target="tpu_custom_call" | custom-call | tf_op jit(solution)/shard_map/exchange/pallas_call | solution.py:276
  18.0 0.0 copy-done
  18.1 0.0 copy-done.1
  18.1 2.1 %gradients.1 = (bf16[2304,256]{1,0:T(8,128)(2,1)}, bf16[256,2304]{1,0:T(8,128)(2,1)}) custom-call(bf16[256,32]{1,0:T(8,128)(2,1)S(1)} %get-tuple-element.7.hid_ref, bf16[32,1152]{1,0:T(8,128)(2,1)S(1)} %get-tuple-element.8.resid_ref, bf16[2304,32]{1,0:T(8,128)(2,1)S(1)} %get-tuple-element.9.cent_ref, bf16[256,1152]{1,0:T(8,128)(2,1)S(1)} %get-tuple-element.10.dec_ref, ...), custom_call_target="tpu_custom_call" | custom-call | tf_op jit(solution)/shard_map/gradients/pallas_call | solution.py:308
Async XLA Ops:
  0.6 17.4 %copy-start = (bf16[256,2304]{1,0:T(8,128)(2,1)S(1)}, bf16[256,2304]{1,0:T(8,128)(2,1)}, u32[]{:S(2)}) copy-start(bf16[256,2304]{1,0:T(8,128)(2,1)} %w_ref.1) | copy-start | bytes 3538948
  0.6 17.4 %copy-start.1 = (bf16[32,256]{1,0:T(8,128)(2,1)S(1)}, bf16[32,256]{1,0:T(8,128)(2,1)}, u32[]{:S(2)}) copy-start(bf16[32,256]{1,0:T(8,128)(2,1)} %pre_ref.1) | copy-start | bytes 49156
